TPU v7x, 128 devices: a whole 4x4x4 slice. The times are simulated.
128 devices in a mesh: wide: 16 (over y, x_hi, core), narrow: 8 (over x_lo, z).
Axes of the slice: x: 4 (x_hi: 2, x_lo: 2; x = x_hi * 2 + x_lo), y: 4, z: 4, core: 2. Of those that a mesh axis runs over, the one named last changes fastest.
Arguments:
- patches: bfloat16 [31360, 1024], P(('wide', 'narrow')), may hold values from -6 to 6
- keep: int32 [640, 49], P(('wide', 'narrow')), may hold values from 0 to 1, as said below
- cotangent: bfloat16 [31360, 1024], P(('wide', 'narrow')), may hold values from -6 to 6
- owner_table: int32 [768], replicated, may hold values from 0 to 767, as said below
- master: float32 [768, 128, 128], P(('wide', 'narrow')), may hold values from -0.1875 to 0.1875
- left_stats: float32 [768, 128, 128], P(('wide', 'narrow'))
- right_stats: float32 [768, 128, 128], P(('wide', 'narrow'))
- left_root: float32 [768, 128, 128], P(('wide', 'narrow'))
- right_root: float32 [768, 128, 128], P(('wide', 'narrow'))
- vectors: float32 [12, 1024], P(None, ('wide', 'narrow'))
- vec_accum: float32 [12, 1024], P(None, ('wide', 'narrow'))
Outputs:
- output: bfloat16 [31360, 1024], P(('wide', 'narrow'))
- input_grad: bfloat16 [31360, 1024], P(('wide', 'narrow'))
- block_grads: float32 [768, 128, 128], P(('wide', 'narrow'))
- new_left: float32 [768, 128, 128], P(('wide', 'narrow'))
- new_right: float32 [768, 128, 128], P(('wide', 'narrow'))
- new_master: float32 [768, 128, 128], P(('wide', 'narrow'))
- new_copy: bfloat16 [768, 128, 128], P(('wide', 'narrow'))
- vec_grads: float32 [12, 1024], P(None, ('wide', 'narrow'))
- vec_accum_new: float32 [12, 1024], P(None, ('wide', 'narrow'))
- vec_new: float32 [12, 1024], P(None, ('wide', 'narrow'))
- grad_norm: float32 [], replicated
Inputs may be any that keep to these rules, and one draw needn't show every extreme that they name: `keep`: each image keeps between 25 and 49 of its patches; the first image keeps exactly 25, the last keeps all. `owner_table`: every block number appears in exactly one slot. A block's class is k * 8 // m, with k its block column and m the block columns of its matrix for Wq, Wk, Wv and W_in, and k its block row and m the block rows of its matrix for Wo and W_out. Slot s holds a block of class (s // 6) % 8.
All inputs are finite; a program needn't handle non-finite values.
Results may differ from a plain program's by a relative error of at most 0.017.
Values may be sent and summed in bfloat16 or wider, within the bound.
A program may use at most 448 MiB of HBM per device.

v0:
```python
import jax
import jax.numpy as jnp
from jax import lax
from jax.sharding import Mesh
from jax.sharding import PartitionSpec as P

HEAD_DIM = 64
FF = 4096
WIDE_NARROW = ("wide_0", "wide_1", "wide_2", "narrow_0", "narrow_1")


highest = lax.Precision.HIGHEST
layer_eps = 1e-05
masked_score = -1000000000.0
decay = 0.5
matrix_rate = 0.5
vector_rate = 0.5
vector_eps = 1e-08


def in_order(pieces, dim):
    pieces = jnp.moveaxis(pieces, 0, dim)
    lengths = pieces.shape
    return pieces.reshape(*lengths[:dim], lengths[dim] * lengths[dim + 1], *lengths[dim + 2 :])


def gather_packed(arrays, axis, dims):
    vector = jnp.concatenate([a.reshape(-1) for a in arrays])
    lines, at, gathered = (lax.all_gather(vector, axis), 0, [])
    for a, dim in zip(arrays, dims):
        pieces = lines[:, at : at + a.size].reshape(-1, *a.shape)
        gathered.append(in_order(pieces, dim))
        at += a.size
    return tuple(gathered)


def in_blocks(shard, dim, count):
    before, after = (shard.shape[:dim], shard.shape[dim + 1 :])
    return jnp.moveaxis(shard.reshape(*before, count, -1, *after), dim, 0)


def one_scatter(arrays, axis, dims):
    count = lax.axis_size(axis)
    pieces = [in_blocks(a, dim, count) for a, dim in zip(arrays, dims)]
    lines = jnp.concatenate([b.reshape(count, -1) for b in pieces], axis=1)
    width = max(16, -(-lines.shape[1] // 1024) * 8)
    lines = jnp.pad(lines, ((0, 0), (0, width * 128 - lines.shape[1]))).reshape(-1, 128)
    vector, at, gathered = (lax.psum_scatter(lines, axis, tiled=True).reshape(-1), 0, [])
    for b in pieces:
        part = b[0]
        gathered.append(vector[at : at + part.size].reshape(part.shape))
        at += part.size
    return tuple(gathered)


def over_axes(shard, axes):
    for axis in axes:
        shard = lax.psum(shard, axis)
    return shard


def layer_norm(values, gain, shift):
    centre = jnp.mean(values, -1, keepdims=True)
    centred = values - centre
    spread = jnp.mean(centred * centred, -1, keepdims=True)
    return centred * lax.rsqrt(spread + layer_eps) * gain + shift


def gelu_exact(values):
    return jax.nn.gelu(values, approximate=False)


def softmax_keys(values):
    return jax.nn.softmax(values, axis=-1)


def from_blocks(ordered, shapes, side):
    matrices = []
    offset = 0
    for row_count, col_count in shapes:
        number = row_count // side * (col_count // side)
        segment = ordered[offset : offset + number].reshape(
            row_count // side, col_count // side, side, side
        )
        matrices.append(segment.transpose(0, 2, 1, 3).reshape(row_count, col_count))
        offset += number
    return matrices


def to_blocks(matrices, side):
    segments = []
    for matrix in matrices:
        row_count, col_count = matrix.shape
        segments.append(
            matrix.reshape(row_count // side, side, col_count // side, side)
            .transpose(0, 2, 1, 3)
            .reshape(-1, side, side)
        )
    return jnp.concatenate(segments, 0)


def product(left, right):
    return jnp.dot(left, right, preferred_element_type=jnp.float32)


def product_right_t(left, right):
    return jnp.einsum("tj,ij->ti", left, right, preferred_element_type=jnp.float32)


def product_left_t(left, right):
    return jnp.einsum("ti,tj->ij", left, right, preferred_element_type=jnp.float32)


def batched(left, right):
    return jnp.einsum("sij,sjk->sik", left, right, precision=highest)


def gram_left(values):
    return jnp.einsum("sij,skj->sik", values, values, precision=highest)


def gram_right(values):
    return jnp.einsum("sji,sjk->sik", values, values, precision=highest)


def same_rows(values):
    return values


def same_pair(first, second):
    return (first, second)


def layer_pass(tokens, cot_float, cotangent, keep, fore, fetch_back, rows, parts, links):
    share_first, attn_total, share_second, mlp_total, hidden_total, share_mid, first_total = links
    q_bias, v_bias, in_bias = parts
    w_query, w_key, w_value, w_output, w_in, w_out = fore
    scale = HEAD_DIM ** (-0.5)
    h_first, first_back_fn = jax.vjp(layer_norm, tokens, rows[0], rows[1])
    a_first, keep_all = share_first(h_first.astype(jnp.bfloat16), keep)
    images = keep_all.shape[0]
    patch_count = keep_all.shape[1]
    row_total = a_first.shape[0]
    col_width = w_query.shape[1]
    head_shape = (images, patch_count, col_width // HEAD_DIM, HEAD_DIM)
    key_mask = keep_all[:, None, None, :] > 0
    queries = (product(a_first, w_query) + q_bias).astype(jnp.bfloat16)
    keys = product(a_first, w_key).astype(jnp.bfloat16)
    values = (product(a_first, w_value) + v_bias).astype(jnp.bfloat16)
    q_heads = queries.reshape(head_shape)
    k_heads = keys.reshape(head_shape)
    v_heads = values.reshape(head_shape)
    raw = jnp.einsum("iqhd,ikhd->ihqk", q_heads, k_heads, preferred_element_type=jnp.float32)
    masked = jnp.where(key_mask, raw * scale, masked_score)
    probs, soft_back = jax.vjp(softmax_keys, masked)
    probs_low = probs.astype(jnp.bfloat16)
    attended = jnp.einsum("ihqk,ikhd->iqhd", probs_low, v_heads, preferred_element_type=jnp.float32)
    attended = attended.reshape(row_total, col_width).astype(jnp.bfloat16)
    middle = tokens + (attn_total(product(attended, w_output)) + rows[4])
    h_second, second_back = jax.vjp(layer_norm, middle, rows[5], rows[6])
    a_second, cot_group = share_second(h_second.astype(jnp.bfloat16), cotangent)
    pre_act = product(a_second, w_in) + in_bias
    activated, gelu_back = jax.vjp(gelu_exact, pre_act)
    act_low = activated.astype(jnp.bfloat16)
    output = (middle + (mlp_total(product(act_low, w_out)) + rows[7])).astype(jnp.bfloat16)
    b_query, b_key, b_value, b_output, b_in, b_out = fetch_back()
    g_out_bias = jnp.sum(cot_float, 0)
    g_w_out = product_left_t(act_low, cot_group)
    d_act = product_right_t(cot_group, b_out)
    d_pre = gelu_back(d_act)[0].astype(jnp.bfloat16)
    g_in_bias = jnp.sum(d_pre.astype(jnp.float32), 0)
    g_w_in = product_left_t(a_second, d_pre)
    d_a2 = hidden_total(product_right_t(d_pre, b_in))
    d_mid_part, g_gain_2, g_shift_2 = second_back(d_a2)
    d_mid = cot_float + d_mid_part
    d_mid_low = d_mid.astype(jnp.bfloat16)
    g_o_bias = jnp.sum(d_mid_low.astype(jnp.float32), 0)
    d_mid_group = share_mid(d_mid_low)
    g_w_output = product_left_t(attended, d_mid_group)
    d_att = product_right_t(d_mid_group, b_output).astype(jnp.bfloat16)
    d_att_heads = d_att.reshape(head_shape)
    d_probs = jnp.einsum(
        "iqhd,ikhd->ihqk", d_att_heads, v_heads, preferred_element_type=jnp.float32
    )
    d_masked = soft_back(d_probs)[0]
    d_raw = (jnp.where(key_mask, d_masked, 0.0) * scale).astype(jnp.bfloat16)
    d_q = (
        jnp.einsum("ihqk,ikhd->iqhd", d_raw, k_heads, preferred_element_type=jnp.float32)
        .reshape(row_total, col_width)
        .astype(jnp.bfloat16)
    )
    d_k = (
        jnp.einsum("ihqk,iqhd->ikhd", d_raw, q_heads, preferred_element_type=jnp.float32)
        .reshape(row_total, col_width)
        .astype(jnp.bfloat16)
    )
    d_v = (
        jnp.einsum("ihqk,iqhd->ikhd", probs_low, d_att_heads, preferred_element_type=jnp.float32)
        .reshape(row_total, col_width)
        .astype(jnp.bfloat16)
    )
    g_q_bias = jnp.sum(d_q.astype(jnp.float32), 0)
    g_v_bias = jnp.sum(d_v.astype(jnp.float32), 0)
    g_w_query = product_left_t(a_first, d_q)
    g_w_key = product_left_t(a_first, d_k)
    g_w_value = product_left_t(a_first, d_v)
    d_a1 = first_total(
        product_right_t(d_q, b_query) + product_right_t(d_k, b_key) + product_right_t(d_v, b_value)
    )
    d_in_part, g_gain_1, g_shift_1 = first_back_fn(d_a1)
    input_grad = (d_mid + d_in_part).astype(jnp.bfloat16)
    grads = [g_w_query, g_w_key, g_w_value, g_w_output, g_w_in, g_w_out]
    full_vecs = (g_gain_1, g_shift_1, g_o_bias, g_gain_2, g_shift_2, g_out_bias)
    part_vecs = (g_q_bias, g_v_bias, g_in_bias)
    return (output, input_grad, grads, full_vecs, part_vecs)


def pack_vectors(full_vecs, part_vecs, width):
    gain_one, shift_one, o_bias, gain_two, shift_two, out_bias = full_vecs
    q_bias, v_bias, in_bias = part_vecs
    return jnp.concatenate(
        [
            jnp.stack([gain_one, shift_one, q_bias, v_bias, o_bias, gain_two, shift_two, out_bias]),
            in_bias.reshape(-1, width),
        ],
        0,
    )


def body(
    patches,
    keep,
    cotangent,
    owner_table,
    master,
    left_stats,
    right_stats,
    left_root,
    right_root,
    vectors,
    vec_accum,
):
    side = master.shape[1]
    width = patches.shape[1]
    weight_copy = master.astype(jnp.bfloat16)
    vector_low = vectors.astype(jnp.bfloat16)
    tokens = patches.astype(jnp.float32)
    cot_float = cotangent.astype(jnp.float32)
    full_shapes = [(width, width)] * 4 + [(width, FF), (FF, width)]
    order_back = jnp.argsort(owner_table)

    def every_block():
        return gather_packed((weight_copy, vector_low), WIDE_NARROW, (0, 1))

    gathered, vector_copy = every_block()
    fore = from_blocks(jnp.take(gathered, order_back, axis=0), full_shapes, side)
    rows = vector_copy.astype(jnp.float32)

    def fetch_back():
        again_blocks = every_block()[0]
        return from_blocks(jnp.take(again_blocks, order_back, axis=0), full_shapes, side)

    parts = (rows[2], rows[3], rows[8:].reshape(-1))
    links = (same_pair, same_rows, same_pair, same_rows, same_rows, same_rows, same_rows)
    output, input_grad, grads, full_vecs, part_vecs = layer_pass(
        tokens, cot_float, cotangent, keep, fore, fetch_back, rows, parts, links
    )
    vec_local = pack_vectors(full_vecs, part_vecs, width)
    slotted = jnp.take(to_blocks(grads, side), owner_table, axis=0)
    block_raw, vec_raw = one_scatter((slotted, vec_local), WIDE_NARROW, (0, 1))
    local_squares = jnp.sum(block_raw * block_raw) + jnp.sum(vec_raw * vec_raw)
    total_squares = over_axes(local_squares, WIDE_NARROW)
    grad_norm = jnp.sqrt(total_squares)
    clip = 1.0 / jnp.maximum(grad_norm, 1.0)
    block_grads = clip * block_raw
    new_left = decay * left_stats + (1.0 - decay) * gram_left(block_grads)
    new_right = decay * right_stats + (1.0 - decay) * gram_right(block_grads)
    direction = batched(batched(left_root, block_grads), right_root)
    new_master = master - matrix_rate * direction
    new_copy = new_master.astype(jnp.bfloat16)
    vec_grads = clip * vec_raw
    vec_accum_new = decay * vec_accum + (1.0 - decay) * vec_grads * vec_grads
    vec_new = vectors - vector_rate * vec_grads / (jnp.sqrt(vec_accum_new) + vector_eps)
    return (
        output,
        input_grad,
        block_grads,
        new_left,
        new_right,
        new_master,
        new_copy,
        vec_grads,
        vec_accum_new,
        vec_new,
        grad_norm,
    )


def solution(mesh):
    torus = Mesh(
        mesh.devices.reshape(4, 2, 2, 2, 4), ("wide_0", "wide_1", "wide_2", "narrow_0", "narrow_1")
    )
    placed = (
        P(WIDE_NARROW, None),
        P(WIDE_NARROW, None),
        P(WIDE_NARROW, None),
        P(),
        P(WIDE_NARROW, None, None),
        P(WIDE_NARROW, None, None),
        P(WIDE_NARROW, None, None),
        P(WIDE_NARROW, None, None),
        P(WIDE_NARROW, None, None),
        P(None, WIDE_NARROW),
        P(None, WIDE_NARROW),
    )
    return jax.shard_map(
        body,
        mesh=torus,
        in_specs=placed,
        out_specs=(
            P(WIDE_NARROW, None),
            P(WIDE_NARROW, None),
            P(WIDE_NARROW, None, None),
            P(WIDE_NARROW, None, None),
            P(WIDE_NARROW, None, None),
            P(WIDE_NARROW, None, None),
            P(WIDE_NARROW, None, None),
            P(None, WIDE_NARROW),
            P(None, WIDE_NARROW),
            P(None, WIDE_NARROW),
            P(),
        ),
        check_vma=False,
    )
```

profile of v0, /device:TPU:1, one launch (start us, length us, event | category | flops | bytes accessed | tf_op | source)
XLA Modules:
  0.0 1267.2 jit_solution(7790427353110202741)
XLA Ops:
  9.2 8.4 broadcast.123
  28.7 228.5 %all-reduce.6.cloned.1.call-done = bf16[12595200]{0:T(1024)(128)(2,1)} async-done(((bf16[12595200]{0:T(1024)(128)(2,1)}), bf16[12595200]{0:T(1024)(128)(2,1)}) %all-reduce.6.cloned.1.call-update) | async-done | bytes 25190416
  257.2 53.5 %reshape.334 = bf16[128,98400]{1,0:T(8,128)(2,1)} reshape(bf16[12595200]{0:T(1024)(128)(2,1)} %all-reduce.6.cloned.1.call-done) | data formatting | bytes 50380800 | tf_op jit(solution)/shard_map/all_gather | solution.py:29
  310.7 20.4 %slice.104 = bf16[128,98304]{1,0:T(8,128)(2,1)} slice(bf16[128,98400]{1,0:T(8,128)(2,1)} %reshape.334), slice={[0:128], [0:98304]} | slice | bytes 50331648 | tf_op jit(solution)/shard_map/slice | solution.py:31
  331.9 26.8 %reshape_reshape.2 = bf16[768,128,128]{2,1,0:T(8,128)(2,1)} reshape(bf16[128,98304]{1,0:T(8,128)(2,1)} %slice.104) | data formatting | bytes 50331648 | tf_op jit(solution)/shard_map/reshape;reshape | solution.py:24
  358.7 27.3 %gather_fusion.1 = bf16[768,128,128]{2,1,0:T(8,128)(2,1)} fusion(bf16[768,128,128]{2,1,0:T(8,128)(2,1)} %reshape_reshape.2, s32[1024]{0:T(1024)S(1)} %get-tuple-element.107), kind=kCustom, calls=%fused_computation.clone | custom fusion | bytes 50334720 | tf_op jit(solution)/shard_map/jit(_take)/gather | solution.py:256
  386.0 13.7 %broadcast_select_fusion.1 = bf16[768,128,128]{2,1,0:T(8,128)(2,1)S(1)} fusion(bf16[768,128,128]{2,1,0:T(8,128)(2,1)} %gather_fusion.1, pred[768]{0:T(1024)(128)(4,1)S(1)} %compare_and_fusion), kind=kLoop, calls=%fused_computation.6 | loop fusion | flops 12582912 | bytes 50332416 | tf_op jit(solution)/shard_map/jit(_take)/select_n | solution.py:256
  448.1 12.0 copy.209
  463.2 23.6 %copy.211 = bf16[32,128,8,128]{3,2,1,0:T(8,128)(2,1)} copy(bf16[32,128,8,128]{3,1,2,0:T(8,128)(2,1)} %bitcast.248) | data formatting | bytes 16777216 | tf_op jit(solution)/shard_map/transpose | solution.py:85
  486.9 15.6 %multiply_convert_fusion = (bf16[245,4096]{1,0:T(8,128)(2,1)}, f32[245,4096]{1,0:T(8,128)S(1)}, f32[245,4096]{1,0:T(8,128)S(1)}) fusion(f32[4096]{0:T(1024)S(1)} %add.174, bf16[128,8,32,128]{3,2,1,0:T(8,128)(2,1)} %bitcast.260, f32[245,1024]{1,0:T(8,128)S(1)} %get-tuple-element.92, f32[1024]{0:T(1024)S(1)} %add.171, f32[1024]{0:T(1024)S(1)} %mul.221, ...), kind=kOutput, calls=%fused_computation.27 | convolution fusion | flops 2122695680 | bytes 19453864 | tf_op jit(solution)/shard_map/dot_general | solution.py:103
  507.5 9.7 multiply_reduce_fusion.1
  532.3 8.3 convolution_bitcast_fusion.1
  577.9 18.3 %copy.230 = f32[8,128,32,128]{3,1,2,0:T(8,128)S(1)} copy(f32[8,128,32,128]{3,2,1,0:T(8,128)S(1)} %bitcast.246) | data formatting | bytes 33554432 | tf_op jit(solution)/shard_map/reshape | solution.py:95
  600.2 8.0 copy.281
  608.2 9.6 copy.231
  646.5 35.3 %gather_fusion = f32[768,128,128]{2,1,0:T(8,128)} fusion(f32[768,128,128]{2,1,0:T(8,128)} %constant_dynamic-update-slice_fusion, s32[1024]{0:T(1024)S(1)} %copy-done.36), kind=kCustom, calls=%fused_computation.1 | custom fusion | bytes 100666368 | tf_op jit(solution)/shard_map/jit(_take)/gather | solution.py:269
  681.8 34.4 %broadcast_select_fusion = f32[768,128,128]{2,1,0:T(8,128)} fusion(f32[768,128,128]{2,1,0:T(8,128)} %gather_fusion, pred[768]{0:T(1024)(128)(4,1)S(1)} %copy-done.44), kind=kLoop, calls=%fused_computation.5 | loop fusion | flops 12582912 | bytes 100664064 | tf_op jit(solution)/shard_map/jit(_take)/select_n | solution.py:269
  716.3 38.5 %select_n.30 = f32[128,98304]{1,0:T(8,128)} reshape(f32[768,128,128]{2,1,0:T(8,128)} %broadcast_select_fusion) | data formatting | bytes 100663296 | tf_op jit(solution)/shard_map/jit(_take)/select_n | solution.py:269
  754.8 36.8 %select_maximum_fusion = f32[128,99328]{1,0:T(8,128)} fusion(f32[128,96]{1,0:T(8,128)S(1)} %copy-done.30, f32[128,98304]{1,0:T(8,128)} %select_n.30), kind=kLoop, calls=%fused_computation.3 | loop fusion | flops 50855936 | bytes 101236736 | tf_op jit(solution)/shard_map/concatenate | solution.py:45
  791.6 38.2 %reshape.316 = f32[99328,128]{1,0:T(8,128)} reshape(f32[128,99328]{1,0:T(8,128)} %select_maximum_fusion) | data formatting | bytes 101711872 | tf_op jit(solution)/shard_map/reshape | solution.py:47
  829.9 363.3 %all-reduce.8.cloned.1.call-done = f32[99328,128]{1,0:T(8,128)} async-done(((f32[99328,128]{1,0:T(8,128)}), f32[99328,128]{1,0:T(8,128)}) %all-reduce.8.cloned.1.call-update) | async-done | bytes 50855952
  1205.1 8.4 psum.35
  1219.6 8.5 psum.37
  1239.3 7.9 psum.39
  (279 shorter events, 193.6 us)
Async XLA Ops:
  7.2 1250.5 %copy-start = (f32[6,128,128]{2,1,0:T(8,128)S(1)}, f32[6,128,128]{2,1,0:T(8,128)}, u32[]{:S(2)}) copy-start(f32[6,128,128]{2,1,0:T(8,128)} %param.21) | copy-start | bytes 1179652
  7.2 250.0 %all-reduce.6.cloned.1.call-start = ((), (), s32[]{:S(2)}) async-start(), calls=%async_computation | async-start | bytes 50380800
  22.0 1171.2 %all-reduce.8.cloned.1.call-start = ((), (), s32[]{:S(2)}) async-start(), calls=%async_computation.1 | async-start | bytes 101711872
  27.8 386.7 %copy-start.33 = (f32[245]{0:T(256)}, f32[245]{0:T(256)S(1)}, u32[]{:S(2)}) copy-start(f32[245]{0:T(256)S(1)} %broadcast_multiply_fusion.1) | copy-start | bytes 2944
  28.1 282.7 %copy-start.42 = (f32[245]{0:T(256)}, f32[245]{0:T(256)S(1)}, u32[]{:S(2)}) copy-start(f32[245]{0:T(256)S(1)} %fusion.119) | copy-start | bytes 2944
  28.1 386.4 %copy-start.40 = (f32[245]{0:T(256)}, f32[245]{0:T(256)S(1)}, u32[]{:S(2)}) copy-start(f32[245]{0:T(256)S(1)} %fusion.140) | copy-start | bytes 2944
  28.7 405.6 %copy-start.45 = (pred[5,49]{1,0:T(8,128)(4,1)}, pred[5,49]{1,0:T(8,128)(4,1)S(1)}, u32[]{:S(2)}) copy-start(pred[5,49]{1,0:T(8,128)(4,1)S(1)} %broadcast_compare_fusion) | copy-start | bytes 739
  310.7 20.4 %slice-start = ((bf16[128,98400]{1,0:T(8,128)(2,1)}), bf16[128,96]{1,0:T(8,128)(2,1)S(1)}, s32[]{:S(2)}) async-start(bf16[128,98400]{1,0:T(8,128)(2,1)} %reshape.334), calls=%async_computation.2 | async-start | bytes 65536 | tf_op jit(solution)/shard_map/slice | solution.py:31
  414.8 15.5 %copy-start.25 = (bf16[245,1024]{1,0:T(8,128)(2,1)}, bf16[245,1024]{1,0:T(8,128)(2,1)S(1)}, u32[]{:S(2)}) copy-start(bf16[245,1024]{1,0:T(8,128)(2,1)S(1)} %fusion.117) | copy-start | bytes 1505284
  443.4 17.2 %copy-start.20 = (bf16[245,1024]{1,0:T(8,128)(2,1)}, bf16[245,1024]{1,0:T(8,128)(2,1)S(1)}, u32[]{:S(2)}) copy-start(bf16[245,1024]{1,0:T(8,128)(2,1)S(1)} %convert_element_type.139) | copy-start | bytes 1505284
  448.1 12.4 copy-start.50
  463.0 69.3 %copy-start.3 = (f32[245,1024]{1,0:T(8,128)}, f32[245,1024]{1,0:T(8,128)S(1)}, u32[]{:S(2)}) copy-start(f32[245,1024]{1,0:T(8,128)S(1)} %get-tuple-element.92) | copy-start | bytes 3010564
  486.9 15.6 %copy-start.7 = (bf16[32,128,8,128]{3,2,1,0:T(8,128)(2,1)S(1)}, bf16[32,128,8,128]{3,2,1,0:T(8,128)(2,1)}, u32[]{:S(2)}) copy-start(bf16[32,128,8,128]{3,2,1,0:T(8,128)(2,1)} %copy.211) | copy-start | bytes 25165828
  486.9 15.6 %copy-start.12 = (bf16[245,1024]{1,0:T(8,128)(2,1)S(1)}, bf16[245,1024]{1,0:T(8,128)(2,1)}, u32[]{:S(2)}) copy-start(bf16[245,1024]{1,0:T(8,128)(2,1)} %param.15) | copy-start | bytes 1505284
  507.5 9.7 copy-start.18
  646.5 35.3 %copy-start.44 = (pred[768]{0:T(1024)(128)(4,1)S(1)}, pred[768]{0:T(1024)(128)(4,1)}, u32[]{:S(2)}) copy-start(pred[768]{0:T(1024)(128)(4,1)} %compare_and_fusion.1) | copy-start | bytes 2308
  716.3 38.5 %copy-start.30 = (f32[128,96]{1,0:T(8,128)S(1)}, f32[128,96]{1,0:T(8,128)}, u32[]{:S(2)}) copy-start(f32[128,96]{1,0:T(8,128)} %copy.241) | copy-start | bytes 147460
  829.8 375.2 %copy-start.39 = (f32[12,8]{0,1:T(8,128)S(1)}, f32[12,8]{0,1:T(8,128)}, u32[]{:S(2)}) copy-start(f32[12,8]{0,1:T(8,128)} %param.22) | copy-start | bytes 1156
  829.8 383.6 %copy-start.47 = (f32[12,8]{0,1:T(8,128)S(1)}, f32[12,8]{0,1:T(8,128)}, u32[]{:S(2)}) copy-start(f32[12,8]{0,1:T(8,128)} %param.23) | copy-start | bytes 1156
  829.8 389.7 %copy-start.38 = (f32[1,128,8]{1,2,0:T(8,128)S(1)}, f32[1,128,8]{1,2,0:T(8,128)}, u32[]{:S(2)}) copy-start(f32[1,128,8]{1,2,0:T(8,128)} %get-tuple-element.81) | copy-start | bytes 12292
  829.8 403.1 %copy-start.4 = (f32[245,1024]{1,0:T(8,128)S(1)}, f32[245,1024]{1,0:T(8,128)}, u32[]{:S(2)}) copy-start(f32[245,1024]{1,0:T(8,128)} %copy-done.3) | copy-start | bytes 3010564
  829.8 403.0 %copy-start.27 = (bf16[245,4096]{1,0:T(8,128)(2,1)S(1)}, bf16[245,4096]{1,0:T(8,128)(2,1)}, u32[]{:S(2)}) copy-start(bf16[245,4096]{1,0:T(8,128)(2,1)} %get-tuple-element.71) | copy-start | bytes 6021124
  1239.3 16.5 %copy-start.29 = (f32[6,128,128]{2,1,0:T(8,128)S(1)}, f32[6,128,128]{2,1,0:T(8,128)}, u32[]{:S(2)}) copy-start(f32[6,128,128]{2,1,0:T(8,128)} %param.20) | copy-start | bytes 1179652
  1239.3 18.3 %copy-start.28 = (f32[6,128,128]{2,1,0:T(8,128)S(1)}, f32[6,128,128]{2,1,0:T(8,128)}, u32[]{:S(2)}) copy-start(f32[6,128,128]{2,1,0:T(8,128)} %param.17) | copy-start | bytes 1179652
  (36 other events, 141.4 us)
Sparse Core Ops, SparseCore 0:
  22.1 235.0 all-reduce.5
  829.9 363.1 all-reduce.7
where the time goes:
time: 1280 us; the launch traced here: 1270 us
  waiting for transfers between devices  592 us (46%)
  local copies, waits for them, and re-layouts  424 us (33%)
  other arithmetic  102 us (8%)
  matrix products  95.6 us (7%)
  blocking collectives  35.5 us (3%)
  between operations  18.5 us (1%)
    unnamed x4, waiting for transfers between devices  592 us
    unnamed x142, local copies, waits for them, and re-layouts  56.1 us
    all_gather x1, local copies, waits for them, and re-layouts, gather_packed(): lines, at, gathered = (lax.all_gather(vector, axis), 0, [])  53.5 us
    transpose x6, local copies, waits for them, and re-layouts, from_blocks(): matrices.append(segment.transpose(0, 2, 1, 3).reshape(row_count, col_count))  48.7 us
    select_n x1, local copies, waits for them, and re-layouts, body(): slotted = jnp.take(to_blocks(grads, side), owner_table, axis=0)  38.5 us
    reshape x1, local copies, waits for them, and re-layouts, one_scatter(): jnp.pad(lines, ((0, 0), (0, width * 128 - lines.shape[1]))).reshape(-1, 128)  38.2 us
    concatenate x1, other arithmetic, one_scatter(): lines = jnp.concatenate([b.reshape(count, -1) for b in pieces], axis=1)  36.8 us
    psum x5, blocking collectives, over_axes(): shard = lax.psum(shard, axis)  35.5 us
  transfers between devices with their start and end apart: 2, of which 2 were waited for; matrix products, arithmetic and copies ran while one was open for 0% of the time, Pallas kernels for 0%

commit v1 on v0

v1 whole, which is shorter than its diff:
```python
import functools
import math

import jax
import jax.numpy as jnp
import numpy as np
from jax import lax
from jax.experimental import pallas as pl
from jax.experimental.pallas import tpu as pltpu
from jax.sharding import PartitionSpec as P

MESH = pl.DeviceIdType.MESH
BOTH = ("wide", "narrow")
F32, BF16 = jnp.float32, jnp.bfloat16
MIB = 2**20

D = 1024
FF = 4096
HEADS = 16
HEAD_DIM = 64
PATCHES = 49
IMAGES = 5
TOKENS = IMAGES * PATCHES
ROWS = 256
SIDE = 128
NBLK = 768
NV = 12
LAYER_EPS = 1e-05
MASKED = -1000000000.0
OUTSIDE = -3.0e38
SCALE = HEAD_DIM**-0.5

ORDERS = ((0, 1, 2), (1, 2, 0), (2, 0, 1))
SHARE = (16, 16, 17)
SHARE_FROM = (0, 16, 32)
PART_FROM = (0, 128 * 16, 128 * 32)
ALL_ROWS = 128 * 49
NEXT = (0, 3, 1, 2)

FIRST = (0, 64, 128, 192, 256, 512)
WIDTH = (8, 8, 8, 8, 32, 8)
LEFT_AT = (0, 0, 0, 8, 16, 24)
RIGHT_AT = (0, 8, 16, 24, 32, 64)


def slot_places():
    block_at, vector_at = np.zeros(NBLK, np.int32), np.zeros(128, np.int32)
    for dev in range(128):
        wide, narrow = dev // 8, dev % 8
        core = wide % 2
        pos = (wide // 2 % 2 * 2 + narrow // 4, wide // 4, narrow % 4)
        for p, (a, b, c) in enumerate(ORDERS):
            at = PART_FROM[p] + (((core * 4 + pos[c]) * 4 + pos[b]) * 4 + pos[a]) * SHARE[p]
            block_at[dev * 6 + 2 * p] = at
            block_at[dev * 6 + 2 * p + 1] = at + 8
            if p == 2:
                vector_at[dev] = at + 16
    return block_at, vector_at


BLOCK_AT, VECTOR_AT = slot_places()


def place():
    wide, narrow = lax.axis_index("wide"), lax.axis_index("narrow")
    x = (wide // 2) % 2 * 2 + narrow // 4
    return (x, wide // 4, narrow % 4), wide % 2


def device(pos, core):
    x, y, z = pos
    return ((y * 2 + x // 2) * 2 + core, x % 2 * 4 + z)


def moved(pos, axis, by):
    return tuple((c + by) % 4 if a == axis else c for a, c in enumerate(pos))


def greet(partners):
    barrier = pltpu.get_barrier_semaphore()
    for partner in partners:
        pl.semaphore_signal(barrier, inc=1, device_id=partner, device_id_type=MESH)
    pl.semaphore_wait(barrier, len(partners))


def loop(count, body):
    lax.fori_loop(0, count, lambda i, _: (body(i), None)[1], None)


def dot(left, right):
    return jnp.dot(left, right, preferred_element_type=F32)


def dot_nt(left, right):
    return lax.dot_general(left, right, (((1,), (1,)), ((), ())), preferred_element_type=F32)


def dot_tn(left, right):
    return lax.dot_general(left, right, (((0,), (0,)), ((), ())), preferred_element_type=F32)


def gather_weights(shard, g, local_sem, send_sem, recv_sem):
    pos, core = place()
    twin = device(pos, 1 - core)
    near = {(a, s): device(moved(pos, a, s), core) for a in range(3) for s in (1, -1)}
    greet([twin] + list(near.values()))
    sends = []

    def copy_of(src, dst, p, slot, to):
        return pltpu.make_async_remote_copy(
            src_ref=src, dst_ref=dst, send_sem=send_sem.at[p, slot],
            recv_sem=recv_sem.at[p, slot], device_id=to, device_id_type=MESH,
        )

    def send(src, dst, p, slot, to):
        copy = copy_of(src, dst, p, slot, to)
        copy.start()
        sends.append(copy)

    def arrived(dst, p, slot):
        copy_of(dst, dst, p, slot, twin).wait_recv()

    def at(p, of_core, c, b, a=0, count=4, skip=0, rows=None):
        start = PART_FROM[p] + (((of_core * 4 + c % 4) * 4 + b % 4) * 4 + a % 4) * SHARE[p] + skip
        return g.at[pl.ds(start, count * SHARE[p] if rows is None else rows)]

    def spot(p):
        a, b, c = ORDERS[p]
        return pos[a], pos[b], pos[c]

    def row(p, ci, bi):
        _, b, c = spot(p)
        return at(p, core, c + ci, b + bi)

    def half_row(p, ci, bi, second):
        _, b, c = spot(p)
        return at(p, core, c + ci, b + bi, 2 if second else 0, 2)

    def chunk(p, ai):
        a, b, c = spot(p)
        return at(p, core, c, b, a + ai, 1)

    def half_chunk(p, ai, second):
        a, b, c = spot(p)
        return at(p, core, c, b, a + ai, 1, 8 if second else 0, SHARE[p] - 8 if second else 8)

    def to_twin(p, ci, bi):
        r = row(p, ci, bi)
        send(r, r, p, 24 + 4 * (ci % 4) + bi % 4, twin)

    def onward(p, base, axis, half):
        first, second = half(False), half(True)
        return (
            lambda: send(first, first, p, base + 2, near[axis, 1]),
            lambda: send(second, second, p, base + 3, near[axis, -1]),
        )

    def both(p, base, axis, src, dst):
        send(src, dst, p, base, near[axis, 1])
        send(src, dst, p, base + 1, near[axis, -1])

    parts = range(3)
    held = []
    for p in parts:
        own = shard.at[pl.ds(SHARE_FROM[p], SHARE[p])]
        both(p, 0, ORDERS[p][0], own, chunk(p, 0))
        copy = pltpu.make_async_copy(own, chunk(p, 0), local_sem.at[p])
        copy.start()
        held.append(copy)
    for p in parts:
        axis = ORDERS[p][0]
        arrived(chunk(p, -1), p, 0)
        onward(p, 0, axis, lambda second: half_chunk(p, -1, second))[0]()
        arrived(chunk(p, 1), p, 1)
        onward(p, 0, axis, lambda second: half_chunk(p, 1, second))[1]()
    for p in parts:
        held[p].wait()
        arrived(half_chunk(p, 2, False), p, 2)
        arrived(half_chunk(p, 2, True), p, 3)
        r = row(p, 0, 0)
        both(p, 4, ORDERS[p][1], r, r)
        both(p, 8, ORDERS[p][2], r, r)
        to_twin(p, 0, 0)
    for p in parts:
        for bi, i in ((-1, 1), (1, 2)):
            r = row(p, 0, bi)
            arrived(r, p, 4 + (i - 1))
            onward(p, 4, ORDERS[p][1], lambda second: half_row(p, 0, bi, second))[i - 1]()
            both(p, 8 + 4 * i, ORDERS[p][2], r, r)
            to_twin(p, 0, bi)

    def sides(p, i):
        bi = NEXT[i]
        for ci, j in ((-1, 0), (1, 1)):
            arrived(row(p, ci, bi), p, 8 + 4 * i + j)
            onward(p, 8 + 4 * i, ORDERS[p][2], lambda second: half_row(p, ci, bi, second))[j]()
            to_twin(p, ci, bi)

    def opposite(p, i):
        bi = NEXT[i]
        arrived(half_row(p, 2, bi, False), p, 8 + 4 * i + 2)
        arrived(half_row(p, 2, bi, True), p, 8 + 4 * i + 3)
        to_twin(p, 2, bi)

    for p in parts:
        sides(p, 0)
    for p in parts:
        arrived(half_row(p, 0, 2, False), p, 6)
        arrived(half_row(p, 0, 2, True), p, 7)
        r = row(p, 0, 2)
        both(p, 8 + 12, ORDERS[p][2], r, r)
        to_twin(p, 0, 2)
    for p in parts:
        sides(p, 1)
        sides(p, 2)
    for p in parts:
        opposite(p, 0)
    for p in parts:
        sides(p, 3)
    for p in parts:
        opposite(p, 1)
        opposite(p, 2)
    for p in parts:
        opposite(p, 3)
    for p in parts:
        _, b, c = spot(p)
        for ci in range(4):
            for bi in range(4):
                arrived(at(p, 1 - core, c + ci, b + bi), p, 24 + 4 * ci + bi)
    return sends


def normal(values):
    centre = jnp.mean(values, -1, keepdims=True)
    centred = values - centre
    spread = jnp.mean(centred * centred, -1, keepdims=True)
    scale = lax.rsqrt(spread + LAYER_EPS)
    return centred * scale, scale


def by_eights(values):
    return jnp.sum(values.reshape(values.shape[0] // 8, 8, values.shape[1]), 0)


def pass_kernel(
    block_at, shard, patches, keep, cotangent,
    output, input_grad, left_out, right_out, vec_out,
    g, left, right, q, k, v, att, a_low, d_att, probs, tokens, mid, d_mid, d_a, act, wall, sums, vec,
    local_sem, send_sem, recv_sem, out_sem,
):
    sends = gather_weights(shard, g, local_sem, send_sem, recv_sem)

    def block(n):
        return g[pl.ds(block_at[n], 8)].reshape(SIDE, SIDE)

    def columns(m, j, count):
        rows = (256 if m == 4 else 64 if m < 4 else 256) // WIDTH[m]
        return jnp.concatenate(
            [
                jnp.concatenate([block(FIRST[m] + r * WIDTH[m] + j + i) for i in range(count)], 1)
                for r in range(rows)
            ],
            0,
        )

    def rows_of(m, i, count):
        return jnp.concatenate(
            [
                jnp.concatenate([block(FIRST[m] + (i + r) * WIDTH[m] + c) for c in range(WIDTH[m])], 1)
                for r in range(count)
            ],
            0,
        )

    def lanes(i, width):
        return pl.ds(pl.multiple_of(i * width, width), width)

    def strip(i):
        return pl.ds(pl.multiple_of(i * 32, 32), 32)

    def stack(first, count):
        return jnp.concatenate([right[first + i] for i in range(count)], 1)

    def line(i):
        return vec[i : i + 1, :]

    def add_sums(i, value, where=slice(None)):
        sums[i, :, where] += by_eights(value)

    for w in range(8):
        window = sum(
            g[int(VECTOR_AT[16 * w + i])].astype(F32) for i in range(16)
        )
        vec[:, w * 128 : (w + 1) * 128] = window
    sums[...] = jnp.zeros_like(sums)

    tokens[0:TOKENS, :] = patches[...].astype(F32)
    tokens[TOKENS:ROWS, :] = jnp.zeros((ROWS - TOKENS, D), F32)
    d_mid[0:TOKENS, :] = cotangent[...].astype(F32)
    d_mid[TOKENS:ROWS, :] = jnp.zeros((ROWS - TOKENS, D), F32)

    row_at = lax.broadcasted_iota(jnp.int32, (ROWS, ROWS), 0)
    col_at = lax.broadcasted_iota(jnp.int32, (ROWS, ROWS), 1)

    def image(at):
        return sum((at >= PATCHES * (i + 1)).astype(jnp.int32) for i in range(IMAGES))

    kept = jnp.broadcast_to(keep[...], (ROWS, ROWS))
    wall[...] = jnp.where(
        image(row_at) == image(col_at), jnp.where(kept > 0, 0.0, MASKED), OUTSIDE
    )

    def first_norm(i):
        n, _ = normal(tokens[strip(i), :])
        a_low[strip(i), :] = (n * line(0) + line(1)).astype(BF16)
        cot = d_mid[strip(i), :]
        for c in range(8):
            right[64 + c, strip(i), :] = cot[:, c * 128 : (c + 1) * 128].astype(BF16)
        add_sums(7, cot)

    loop(8, first_norm)

    def project(j):
        left[pl.ds(2 * j, 2)] = a_low[:, lanes(j, 256)].T.reshape(2, 128, ROWS)
        at = lanes(j, 256)
        q[:, at] = (dot(a_low[...], columns(0, 2 * j, 2)) + vec[2:3, at]).astype(BF16)
        k[:, at] = dot(a_low[...], columns(1, 2 * j, 2)).astype(BF16)
        v[:, at] = (dot(a_low[...], columns(2, 2 * j, 2)) + vec[3:4, at]).astype(BF16)

    loop(4, project)

    low_half = lax.broadcasted_iota(jnp.int32, (ROWS, 128), 1) < HEAD_DIM

    def split(pair):
        nothing = jnp.zeros_like(pair)
        return jnp.where(low_half, pair, nothing), jnp.where(low_half, nothing, pair)

    def attend(j):
        at = lanes(j, 128)
        kp = k[:, at]
        weights = []
        for h, qh in enumerate(split(q[:, at])):
            raw = dot_nt(qh, kp)
            masked = jnp.where(wall[...] == 0.0, raw * SCALE, wall[...])
            e = jnp.exp(masked - jnp.max(masked, -1, keepdims=True))
            p = e / jnp.sum(e, -1, keepdims=True)
            probs[2 * j + h] = p
            weights.append(p.astype(BF16))
        pair = dot(jnp.concatenate(weights, 1), jnp.concatenate(split(v[:, at]), 0)).astype(BF16)
        att[:, at] = pair
        left[8 + j] = pair.T

    loop(8, attend)

    def to_mid(j):
        at = lanes(j, 256)
        mid[:, at] = tokens[:, at] + (dot(att[...], columns(3, 2 * j, 2)) + vec[4:5, at])

    loop(4, to_mid)

    def second_norm(i):
        n, _ = normal(mid[strip(i), :])
        a_low[strip(i), :] = (n * line(5) + line(6)).astype(BF16)

    loop(8, second_norm)

    def hidden(j):
        pre = dot(a_low[...], columns(4, 2 * j, 2)) + vec[pl.ds(8 + j // 4, 1), lanes(j % 4, 256)]
        half = 0.5 * (1.0 + lax.erf(pre * math.sqrt(0.5)))
        slope = half + pre * (jnp.exp(-0.5 * pre * pre) * (1.0 / math.sqrt(2.0 * math.pi)))
        low = (pre * half).astype(BF16)
        act[:, lanes(j, 256)] = low
        left[pl.ds(24 + 2 * j, 2)] = low.T.reshape(2, 128, ROWS)
        d_pre = (dot_nt(stack(64, 8), rows_of(5, 2 * j, 2)) * slope).astype(BF16)
        right[32 + 2 * j] = d_pre[:, :128]
        right[33 + 2 * j] = d_pre[:, 128:]
        add_sums(8 + j // 4, d_pre.astype(F32), lanes(j % 4, 256))

    loop(16, hidden)

    def second_back(j):
        at = lanes(j, 256)
        left[pl.ds(16 + 2 * j, 2)] = a_low[:, at].T.reshape(2, 128, ROWS)
        d_a[:, at] = dot_nt(stack(32, 32), rows_of(4, 2 * j, 2))

    loop(4, second_back)

    def mid_back(i):
        rows = strip(i)
        n, scale = normal(mid[rows, :])
        d = d_a[rows, :]
        e = d * line(5)
        inner = e - jnp.mean(e, -1, keepdims=True) - n * jnp.mean(e * n, -1, keepdims=True)
        whole = d_mid[rows, :] + inner * scale
        d_mid[rows, :] = whole
        low = whole.astype(BF16)
        for c in range(8):
            right[24 + c, rows, :] = low[:, c * 128 : (c + 1) * 128]
        add_sums(5, d * n)
        add_sums(6, d)
        add_sums(4, low.astype(F32))

    loop(8, mid_back)

    def att_back(j):
        d_att[:, lanes(j, 256)] = dot_nt(stack(24, 8), rows_of(3, 2 * j, 2)).astype(BF16)

    loop(4, att_back)

    def heads_back(j):
        at = lanes(j, 128)
        vp = v[:, at]
        q_parts, k_parts, da_parts = split(q[:, at]), split(k[:, at]), split(d_att[:, at])
        d_raws, weights = [], []
        for h in range(2):
            p = probs[2 * j + h]
            d_p = dot_nt(da_parts[h], vp)
            d_m = p * (d_p - jnp.sum(p * d_p, -1, keepdims=True))
            d_raws.append(jnp.where(wall[...] == 0.0, d_m * SCALE, 0.0).astype(BF16))
            weights.append(p.astype(BF16))
        d_q = dot(jnp.concatenate(d_raws, 1), jnp.concatenate(k_parts, 0)).astype(BF16)
        d_k = dot_tn(jnp.concatenate(d_raws, 0), jnp.concatenate(q_parts, 0)).astype(BF16)
        d_v = dot_tn(jnp.concatenate(weights, 0), jnp.concatenate(da_parts, 0)).astype(BF16)
        right[j] = d_q
        right[8 + j] = d_k
        right[16 + j] = d_v
        add_sums(2, d_q.astype(F32), at)
        add_sums(3, d_v.astype(F32), at)

    loop(8, heads_back)

    copies = [
        pltpu.make_async_copy(left, left_out, out_sem.at[0]),
        pltpu.make_async_copy(right, right_out, out_sem.at[1]),
    ]
    for copy in copies:
        copy.start()

    def first_back(j):
        weights = jnp.concatenate([rows_of(m, 2 * j, 2) for m in range(3)], 1)
        d_a[:, lanes(j, 256)] = dot_nt(stack(0, 24), weights)

    loop(4, first_back)

    def token_back(i):
        rows = strip(i)
        n, scale = normal(tokens[rows, :])
        d = d_a[rows, :]
        e = d * line(0)
        inner = e - jnp.mean(e, -1, keepdims=True) - n * jnp.mean(e * n, -1, keepdims=True)
        d_mid[rows, :] = d_mid[rows, :] + inner * scale
        add_sums(0, d * n)
        add_sums(1, d)

    loop(8, token_back)
    input_grad[...] = d_mid[0:TOKENS, :].astype(BF16)

    def last(j):
        at = lanes(j, 256)
        d_a[:, at] = mid[:, at] + (dot(act[...], columns(5, 2 * j, 2)) + vec[7:8, at])

    loop(4, last)
    output[...] = d_a[0:TOKENS, :].astype(BF16)
    vec_out[0:NV, :] = jnp.sum(sums[...], 1)
    vec_out[NV:, :] = jnp.zeros((16 - NV, D), F32)
    for copy in copies:
        copy.wait()
    for copy in sends:
        copy.wait_send()


def forward_backward(block_at, shard, patches, keep, cotangent):
    anywhere, vmem = pl.BlockSpec(memory_space=pl.ANY), pl.BlockSpec(memory_space=pltpu.VMEM)
    flat = (ROWS, D)
    return pl.pallas_call(
        pass_kernel,
        out_shape=[
            jax.ShapeDtypeStruct((TOKENS, D), BF16),
            jax.ShapeDtypeStruct((TOKENS, D), BF16),
            jax.ShapeDtypeStruct((56, 128, ROWS), BF16),
            jax.ShapeDtypeStruct((72, ROWS, 128), BF16),
            jax.ShapeDtypeStruct((16, D), F32),
        ],
        in_specs=[pl.BlockSpec(memory_space=pltpu.SMEM), anywhere, vmem, vmem, vmem],
        out_specs=[vmem, vmem, anywhere, anywhere, vmem],
        scratch_shapes=[
            pltpu.VMEM((ALL_ROWS, 16, 128), BF16),
            pltpu.VMEM((56, 128, ROWS), BF16),
            pltpu.VMEM((72, ROWS, 128), BF16),
            pltpu.VMEM(flat, BF16),
            pltpu.VMEM(flat, BF16),
            pltpu.VMEM(flat, BF16),
            pltpu.VMEM(flat, BF16),
            pltpu.VMEM(flat, BF16),
            pltpu.VMEM(flat, BF16),
            pltpu.VMEM((HEADS, ROWS, ROWS), F32),
            pltpu.VMEM(flat, F32),
            pltpu.VMEM(flat, F32),
            pltpu.VMEM(flat, F32),
            pltpu.VMEM(flat, F32),
            pltpu.VMEM((ROWS, FF), BF16),
            pltpu.VMEM((ROWS, ROWS), F32),
            pltpu.VMEM((NV, 8, D), F32),
            pltpu.VMEM((16, D), F32),
            pltpu.SemaphoreType.DMA((3,)),
            pltpu.SemaphoreType.DMA((3, 40)),
            pltpu.SemaphoreType.DMA((3, 40)),
            pltpu.SemaphoreType.DMA((2,)),
        ],
        compiler_params=pltpu.CompilerParams(
            collective_id=0, has_side_effects=True, vmem_limit_bytes=62 * MIB
        ),
        cost_estimate=pl.CostEstimate(
            flops=13_000_000_000, bytes_accessed=60_000_000, transcendentals=3_000_000
        ),
        name="forward_backward",
    )(block_at, shard, patches, keep, cotangent)


AHEAD = 3


def scatter_kernel(
    left_at, right_at, left, right, vec_in,
    total, window, norm_tile,
    tw_out, tw_in, c_out, c_in, c_half, b_out, b_in, b_half, a_out, a_in, a_half, kept, vec, vec_in_buf, tiles, mask,
    tw_send, tw_recv, c_send, c_recv, b_send, b_recv, a_send, a_recv, v_send, v_recv, n_send, n_recv,
):
    pos, core = place()
    twin = device(pos, 1 - core)
    axes = [[device(moved(pos, a, s), core) for s in (1, 2, 3)] for a in range(3)]
    greet([twin] + [to for three in axes for to in three])

    def pick(options, i):
        value = options[-1]
        for n in range(len(options) - 2, -1, -1):
            value = jnp.where(i == n, options[n], value)
        return value

    def axis_of(p, which):
        return lax.rem(p + which, 3)

    def neighbour(p, which, by):
        axis = axis_of(p, which)
        if isinstance(by, int):
            return tuple(pick([axes[a][by - 1][n] for a in range(3)], axis) for n in range(2))
        ahead, back = neighbour(p, which, 1), neighbour(p, which, 3)
        return tuple(jnp.where(by == 1, ahead[n], back[n]) for n in range(2))

    def along(p, which, by):
        return lax.rem(pick(pos, axis_of(p, which)) + by, 4)

    def pair(p, ci, bi, ai, of_core):
        spots = [along(p, 0, ai), along(p, 1, bi), along(p, 2, ci)]
        x, y, z = (pick([spots[(a - s) % 3] for s in range(3)], p) for a in range(3))
        wide, narrow = device((x, y, z), of_core)
        slot = (wide * 8 + narrow) * 6 + 2 * p
        made = []
        for i in range(2):
            made.append(dot(left[left_at[slot + i]], right[right_at[slot + i]]))
        return jnp.concatenate(made, 0)

    def order(i):
        return pick([2, 1, 3, 0], i)

    def step(s):
        quarter, p = s // 3, lax.rem(s, 3)
        ci = jnp.where(quarter < 4, 2, jnp.where(quarter < 12, jnp.where(lax.rem(quarter, 2) == 0, 1, 3), 0))
        i = jnp.where(quarter < 4, quarter, jnp.where(quarter < 12, (quarter - 4) // 2, quarter - 12))
        return p, ci, order(i)

    def remote(src, dst, send_sem, recv_sem, to):
        return pltpu.make_async_remote_copy(
            src_ref=src, dst_ref=dst, send_sem=send_sem, recv_sem=recv_sem, device_id=to, device_id_type=MESH
        )

    def twin_copy(p, ci, bi):
        n = p * 16 + ci * 4 + bi
        return remote(tw_out.at[n], tw_in.at[n], tw_send.at[n], tw_recv.at[n], twin)

    def for_twin(s):
        p, ci, bi = step(s)
        for ai in range(4):
            tw_out[p * 16 + ci * 4 + bi, ai] = pair(p, ci, bi, ai, 1 - core).astype(BF16)
        twin_copy(p, ci, bi).start()

    def chip_sum(p, ci, bi, ai):
        return pair(p, ci, bi, ai, core) + tw_in[p * 16 + ci * 4 + bi, ai].astype(F32)

    def c_half_copy(p, bi, second):
        n = p * 4 + bi
        part = pl.ds(2 if second else 0, 2)
        return remote(
            c_out.at[n, part], c_half.at[n, part], c_send.at[2 * n + second], c_recv.at[2 * n + second],
            neighbour(p, 2, 3 if second else 1),
        )

    def c_whole_copy(p, bi, leftward):
        n = p * 4 + bi
        return remote(
            c_out.at[12 + 12 * leftward + n], c_in.at[12 * leftward + n], c_send.at[24 + 12 * leftward + n],
            c_recv.at[24 + 12 * leftward + n], neighbour(p, 2, 1 + 2 * leftward),
        )

    def b_half_copy(p, second):
        part = pl.ds(2 if second else 0, 2)
        return remote(
            b_out.at[p, 0, part], b_half.at[p, part], b_send.at[4 * p + second], b_recv.at[4 * p + second],
            neighbour(p, 1, 3 if second else 1),
        )

    def b_whole_copy(p, leftward):
        return remote(
            b_out.at[p, 1 + leftward], b_in.at[p, leftward], b_send.at[4 * p + 2 + leftward],
            b_recv.at[4 * p + 2 + leftward], neighbour(p, 1, 3 if leftward else 1),
        )

    def a_half_copy(p, second):
        part = pl.ds(128 if second else 0, 128)
        return remote(
            a_out.at[p, 0, part], a_half.at[p, part], a_send.at[4 * p + second], a_recv.at[4 * p + second],
            neighbour(p, 0, 3 if second else 1),
        )

    def a_whole_copy(p, leftward):
        return remote(
            a_out.at[p, 1 + leftward], a_in.at[p, leftward], a_send.at[4 * p + 2 + leftward],
            a_recv.at[4 * p + 2 + leftward], neighbour(p, 0, 3 if leftward else 1),
        )

    def vec_twin():
        return remote(vec.at[0], vec_in_buf.at[0], v_send.at[0], v_recv.at[0], twin)

    def vec_copy(axis, by):
        n = 1 + 3 * axis + by - 1
        return remote(vec.at[1 + axis], vec_in_buf.at[n], v_send.at[n], v_recv.at[n], axes[axis][by - 1])

    def vec_axis(axis):
        if axis == 0:
            vec_twin().wait_recv()
            vec[1] = vec[0] + vec_in_buf[0]
        else:
            vec[1 + axis] = vec_done(axis - 1)
        for by in (1, 2, 3):
            vec_copy(axis, by).start()

    def vec_done(axis):
        whole = vec[1 + axis]
        for by in (1, 2, 3):
            vec_copy(axis, by).wait_recv()
            whole = whole + vec_in_buf[3 * axis + by]
        return whole

    vec[0] = vec_in[...]
    vec_twin().start()

    loop(AHEAD, for_twin)

    def opposite_step(s):
        for_twin(s + AHEAD)
        p, ci, bi = step(s)
        n = p * 4 + bi
        twin_copy(p, ci, bi).wait_recv()
        for ai in range(4):
            c_out[n, ai] = chip_sum(p, ci, bi, ai).astype(BF16)
        c_half_copy(p, bi, 0).start()
        c_half_copy(p, bi, 1).start()

    loop(12, opposite_step)
    vec_axis(0)

    def side_step(s):
        p, ci, bi = step(s)
        leftward = jnp.where(ci == 3, 1, 0)
        n = p * 4 + bi
        out = 12 + 12 * leftward + n
        twin_copy(p, ci, bi).wait_recv()
        remote(
            c_out.at[n, pl.ds(0, 2)], c_half.at[n, pl.ds(2 * leftward, 2)], c_send.at[2 * n + leftward],
            c_recv.at[2 * n + leftward], twin,
        ).wait_recv()
        for i in range(2):
            ai = 2 * leftward + i
            c_out[out, ai] = (chip_sum(p, ci, bi, ai) + c_half[n, ai].astype(F32)).astype(BF16)
        for i in range(2):
            ai = 2 - 2 * leftward + i
            c_out[out, ai] = chip_sum(p, ci, bi, ai).astype(BF16)
        c_whole_copy(p, bi, leftward).start()

    def side_ahead(i):
        for_twin(12 + i + AHEAD)
        side_step(12 + i)

    loop(24, side_ahead)
    vec_axis(1)

    def own_sum(p, bi, ai):
        n = p * 4 + bi
        return chip_sum(p, 0, bi, ai) + c_in[n, ai].astype(F32) + c_in[12 + n, ai].astype(F32)

    def own_arrived(p, bi):
        twin_copy(p, 0, bi).wait_recv()
        c_whole_copy(p, bi, 0).wait_recv()
        c_whole_copy(p, bi, 1).wait_recv()

    def b_opposite(p):
        for_twin(36 + p + AHEAD)
        own_arrived(p, 2)
        for ai in range(4):
            b_out[p, 0, ai] = own_sum(p, 2, ai).astype(BF16)
        b_half_copy(p, 0).start()
        b_half_copy(p, 1).start()

    loop(3, b_opposite)

    def b_side(leftward):
        def body(p):
            for_twin(39 + 3 * leftward + p + AHEAD)
            bi = 3 if leftward else 1
            own_arrived(p, bi)
            b_half_copy(p, leftward).wait_recv()
            for ai in range(4):
                value = own_sum(p, bi, ai)
                if ai // 2 == leftward:
                    value = value + b_half[p, ai].astype(F32)
                b_out[p, 1 + leftward, ai] = value.astype(BF16)
            b_whole_copy(p, leftward).start()

        return body

    loop(3, b_side(0))
    loop(3, b_side(1))

    def b_own(p):
        own_arrived(p, 0)
        for ai in range(4):
            kept[p, ai] = own_sum(p, 0, ai)

    loop(3, b_own)

    def row_sum(p, ai):
        return kept[p, ai] + b_in[p, 0, ai].astype(F32) + b_in[p, 1, ai].astype(F32)

    def a_opposite(p):
        b_whole_copy(p, 0).wait_recv()
        b_whole_copy(p, 1).wait_recv()
        a_out[p, 0] = row_sum(p, 2).astype(BF16)
        a_half_copy(p, 0).start()
        a_half_copy(p, 1).start()

    loop(3, a_opposite)
    vec_axis(2)

    def a_sides(p):
        for leftward in (0, 1):
            a_half_copy(p, leftward).wait_recv()
            value = row_sum(p, 3 if leftward else 1)
            at = slice(128, 256) if leftward else slice(0, 128)
            other = slice(0, 128) if leftward else slice(128, 256)
            a_out[p, 1 + leftward, at] = (value[at] + a_half[p, at].astype(F32)).astype(BF16)
            a_out[p, 1 + leftward, other] = value[other].astype(BF16)
            a_whole_copy(p, leftward).start()

    loop(3, a_sides)

    squares = jnp.zeros((8, 128), F32)
    for p in range(3):
        a_whole_copy(p, 0).wait_recv()
        a_whole_copy(p, 1).wait_recv()
        value = row_sum(p, 0) + a_in[p, 0].astype(F32) + a_in[p, 1].astype(F32)
        total[2 * p] = value[:128]
        total[2 * p + 1] = value[128:]
        squares = squares + by_eights(value * value)

    wide, narrow = lax.axis_index("wide"), lax.axis_index("narrow")
    vec[4] = vec_done(2)
    mine = vec[4, :, pl.ds(pl.multiple_of((wide // 2) * 128, 128), 128)]
    window[...] = mine
    lane = lax.broadcasted_iota(jnp.int32, (16, 128), 1) // 8
    own = jnp.where(lane == lax.rem(wide, 2) * 8 + narrow, mine, 0.0)
    squares = squares + by_eights(own * own)

    tiles[0] = squares

    def norm_copy(stage, by):
        n = 1 + 3 * (stage - 1) + by - 1 if stage else 0
        to = axes[stage - 1][by - 1] if stage else twin
        return remote(tiles.at[stage], tiles.at[5 + n], n_send.at[n], n_recv.at[n], to)

    for stage in range(4):
        partners = (1, 2, 3) if stage else (1,)
        for by in partners:
            norm_copy(stage, by).start()
        whole = tiles[stage]
        for by in partners:
            norm_copy(stage, by).wait_recv()
            whole = whole + tiles[5 + (1 + 3 * (stage - 1) + by - 1 if stage else 0)]
        tiles[stage + 1] = whole
    norm_tile[...] = tiles[4]

    def sent(s):
        p, ci, bi = step(s)
        twin_copy(p, ci, bi).wait_send()

    loop(48, sent)

    def sent_along(p):
        for bi in range(4):
            for side in (0, 1):
                c_half_copy(p, bi, side).wait_send()
                c_whole_copy(p, bi, side).wait_send()
        for side in (0, 1):
            b_half_copy(p, side).wait_send()
            b_whole_copy(p, side).wait_send()
            a_half_copy(p, side).wait_send()
            a_whole_copy(p, side).wait_send()

    loop(3, sent_along)
    vec_twin().wait_send()
    norm_copy(0, 1).wait_send()
    for axis in range(3):
        for by in (1, 2, 3):
            vec_copy(axis, by).wait_send()
            norm_copy(axis + 1, by).wait_send()


def sum_gradients(left_at, right_at, left, right, vec):
    smem, vmem = pl.BlockSpec(memory_space=pltpu.SMEM), pl.BlockSpec(memory_space=pltpu.VMEM)
    row = (4, 256, 128)
    dma = pltpu.SemaphoreType.DMA
    return pl.pallas_call(
        scatter_kernel,
        out_shape=[
            jax.ShapeDtypeStruct((6, SIDE, SIDE), F32),
            jax.ShapeDtypeStruct((16, 128), F32),
            jax.ShapeDtypeStruct((8, 128), F32),
        ],
        in_specs=[smem, smem, vmem, vmem, vmem],
        out_specs=[vmem, vmem, vmem],
        scratch_shapes=[
            pltpu.VMEM((48, *row), BF16),
            pltpu.VMEM((48, *row), BF16),
            pltpu.VMEM((36, *row), BF16),
            pltpu.VMEM((24, *row), BF16),
            pltpu.VMEM((12, *row), BF16),
            pltpu.VMEM((3, 3, *row), BF16),
            pltpu.VMEM((3, 2, *row), BF16),
            pltpu.VMEM((3, *row), BF16),
            pltpu.VMEM((3, 3, 256, 128), BF16),
            pltpu.VMEM((3, 2, 256, 128), BF16),
            pltpu.VMEM((3, 256, 128), BF16),
            pltpu.VMEM((3, *row), F32),
            pltpu.VMEM((5, 16, D), F32),
            pltpu.VMEM((10, 16, D), F32),
            pltpu.VMEM((15, 8, 128), F32),
            pltpu.VMEM((8, 128), F32),
            dma((48,)), dma((48,)), dma((48,)), dma((48,)), dma((12,)), dma((12,)), dma((12,)), dma((12,)),
            dma((10,)), dma((10,)), dma((10,)), dma((10,)),
        ],
        compiler_params=pltpu.CompilerParams(
            collective_id=1, has_side_effects=True, vmem_limit_bytes=62 * MIB
        ),
        cost_estimate=pl.CostEstimate(
            flops=6_500_000_000, bytes_accessed=10_000_000, transcendentals=0
        ),
        name="sum_gradients",
    )(left_at, right_at, left, right, vec)


def exact(left, right, over):
    return lax.dot_general(
        left, right, (over, ((), ())), precision=lax.Precision.HIGHEST, preferred_element_type=F32
    )


def step_kernel(
    raw, window, norm_tile, place_ref, master, left_stats, right_stats, left_root, right_root, vectors, vec_accum,
    block_grads, new_left, new_right, new_master, new_copy, vec_grads, vec_accum_new, vec_new, grad_norm,
):
    norm = jnp.sqrt(jnp.sum(norm_tile[...], keepdims=True))
    clip = 1.0 / jnp.maximum(norm, 1.0)
    for i in range(raw.shape[0]):
        grads = raw[i] * clip
        block_grads[i] = grads
        new_left[i] = 0.5 * left_stats[i] + 0.5 * exact(grads, grads, ((1,), (1,)))
        new_right[i] = 0.5 * right_stats[i] + 0.5 * exact(grads, grads, ((0,), (0,)))
        way = exact(exact(left_root[i], grads, ((1,), (0,))), right_root[i], ((1,), (0,)))
        master_now = master[i] - 0.5 * way
        new_master[i] = master_now
        new_copy[i] = master_now.astype(BF16)

    @pl.when(pl.program_id(0) == 0)
    def _():
        grad_norm[...] = norm
        mine = pltpu.roll(window[...], place_ref[0], 1)[:NV, :8]
        grads = clip * mine
        vec_grads[...] = grads
        accum = 0.5 * vec_accum[...] + 0.5 * grads * grads
        vec_accum_new[...] = accum
        vec_new[...] = vectors[...] - 0.5 * grads / (jnp.sqrt(accum) + 1e-08)


def update(raw, window, norm_tile, shift, master, left_stats, right_stats, left_root, right_root, vectors, vec_accum):
    per = 2
    blocks = pl.BlockSpec((per, SIDE, SIDE), lambda i: (i, 0, 0))

    def whole(*shape):
        return pl.BlockSpec(shape, lambda i: (0,) * len(shape))

    f32_blocks = jax.ShapeDtypeStruct((6, SIDE, SIDE), F32)
    f32_vecs = jax.ShapeDtypeStruct((NV, 8), F32)
    return pl.pallas_call(
        step_kernel,
        grid=(6 // per,),
        out_shape=[f32_blocks] * 4
        + [jax.ShapeDtypeStruct((6, SIDE, SIDE), BF16)]
        + [f32_vecs] * 3
        + [jax.ShapeDtypeStruct((1, 1), F32)],
        in_specs=[blocks, whole(16, 128), whole(8, 128), pl.BlockSpec(memory_space=pltpu.SMEM)]
        + [blocks] * 5
        + [whole(NV, 8)] * 2,
        out_specs=[blocks] * 5 + [whole(NV, 8)] * 3 + [whole(1, 1)],
        compiler_params=pltpu.CompilerParams(vmem_limit_bytes=32 * MIB),
        name="update",
    )(raw, window, norm_tile, shift, master, left_stats, right_stats, left_root, right_root, vectors, vec_accum)


def body(
    patches, keep, cotangent, owner_table, master, left_stats, right_stats, left_root, right_root, vectors, vec_accum,
):
    wide, narrow = lax.axis_index("wide"), lax.axis_index("narrow")
    lane = ((wide % 2) * 8 + narrow) * 8
    vec_tile = lax.dynamic_update_slice(jnp.zeros((16, 128), BF16), vectors.astype(BF16), (0, lane))
    shard = jnp.concatenate([master.astype(BF16).reshape(48, 16, SIDE), vec_tile[None]], 0)

    numbers = jnp.arange(NBLK, dtype=jnp.int32)
    held = owner_table[None, :] == numbers[:, None]
    block_at = jnp.sum(jnp.where(held, jnp.asarray(BLOCK_AT)[None, :], 0), 1)
    matrix = sum((owner_table >= first).astype(jnp.int32) for first in FIRST[1:])

    def by_matrix(values):
        return sum(jnp.where(matrix == m, value, 0) for m, value in enumerate(values))

    inner = owner_table - by_matrix(FIRST)
    block_row = jnp.where(matrix == 4, inner // 32, inner // 8)
    block_column = jnp.where(matrix == 4, inner % 32, inner % 8)
    left_at = by_matrix(LEFT_AT) + block_row
    right_at = by_matrix(RIGHT_AT) + block_column

    kept = jnp.pad(keep.reshape(1, TOKENS), ((0, 0), (0, ROWS - TOKENS)), constant_values=1)
    output, input_grad, left, right, vec = forward_backward(block_at, shard, patches, kept, cotangent)
    raw, window, norm_tile = sum_gradients(left_at, right_at, left, right, vec)
    shift = jnp.reshape((128 - lane) % 128, (1,)).astype(jnp.int32)
    *rest, grad_norm = update(
        raw, window, norm_tile, shift, master, left_stats, right_stats, left_root, right_root, vectors, vec_accum
    )
    return (output, input_grad, *rest, grad_norm.reshape(()))


def solution(mesh):
    rows, blocks, vecs = P(BOTH, None), P(BOTH, None, None), P(None, BOTH)
    return jax.shard_map(
        body,
        mesh=mesh,
        in_specs=(rows, rows, rows, P(), blocks, blocks, blocks, blocks, blocks, vecs, vecs),
        out_specs=(rows, rows, blocks, blocks, blocks, blocks, blocks, vecs, vecs, vecs, P()),
        check_vma=False,
    )
```

time: 1280 us -> 208 us (0.16)
  waiting for transfers between devices: 592 us -> 0 us
  local copies, waits for them, and re-layouts: 424 us -> 8.17 us
  Pallas kernels: 0 us -> 194 us
  other arithmetic: 102 us -> 4.64 us
  matrix products: 95.6 us -> 0 us
  blocking collectives: 35.5 us -> 0 us
  between operations: 18.5 us -> 0.79 us
    unnamed x4 -> x0, waiting for transfers between devices: 592 us -> none
    pallas_call x0 -> x3, Pallas kernels: none -> 194 us  [the longest x1 107 us: forward_backward(): pl.pallas_call(pass_kernel, out_shape=[jax.ShapeDtypeStruct((TOKENS, D),...]
    dot_general x27 -> x0, matrix products: 92.6 us -> none  [the longest x6 29.8 us: product(): return jnp.dot(left, right, preferred_element_type=jnp.float32)]
    reshape x9 -> x1, local copies, waits for them, and re-layouts: 76 us -> 0.76 us  [body(): keep.reshape(1, TOKENS)]
    gather x2 -> x0, local copies, waits for them, and re-layouts: 62.7 us -> none  [the longest x1 35.3 us: body(): slotted = jnp.take(to_blocks(grads, side), owner_table, axis=0)]
    all_gather x1 -> x0, local copies, waits for them, and re-layouts: 53.5 us -> none  [gather_packed(): lines, at, gathered = (lax.all_gather(vector, axis), 0, [])]
    unnamed x142 -> x33, local copies, waits for them, and re-layouts: 56.1 us -> 6.15 us
    transpose x6 -> x0, local copies, waits for them, and re-layouts: 48.7 us -> none  [from_blocks(): matrices.append(segment.transpose(0, 2, 1, 3).reshape(row_count, col_count))]
  transfers between devices with their start and end apart: 2 -> 0, of which waited for: 2 -> 0; matrix products, arithmetic and copies ran while one was open for 0% -> 0% of each run, Pallas kernels for 0% -> 0%
where the time goes in v1:
time: 208 us; the launch traced here: 207 us
  Pallas kernels  194 us (93%)
  local copies, waits for them, and re-layouts  8.17 us (4%)
  other arithmetic  4.64 us (2%)
    pallas_call x1, Pallas kernels, forward_backward(): pl.pallas_call(pass_kernel, out_shape=[jax.ShapeDtypeStruct((TOKENS, D),...  107 us
    pallas_call x1, Pallas kernels, sum_gradients(): pl.pallas_call(scatter_kernel, out_shape=[jax.ShapeDtypeStruct((6, SIDE,...  82.2 us
    unnamed x33, local copies, waits for them, and re-layouts  6.15 us
    pallas_call x1, Pallas kernels, update(): pl.pallas_call(step_kernel, grid=(6 // per,), out_shape=[f32_blocks] * 4...  4.58 us

profile of v1, /device:TPU:1, one launch (start us, length us, event | category | flops | bytes accessed | tf_op | source)
XLA Modules:
  0.0 207.2 jit_solution(4906668287911373621)
XLA Ops:
  0.7 0.7 convert_bitcast_fusion
  1.4 0.1 copy.29
  1.4 0.6 dynamic_update_slice.4
  2.0 1.0 convert_element_type.21
  3.1 0.7 pad_maximum_fusion.shard
  3.8 1.6 select_reduce_fusion.block_at
  5.4 0.8 reshape.39
  6.1 0.6 pad.4.keep
  6.7 106.8 %forward_backward.1 = (bf16[245,1024]{1,0:T(8,128)(2,1)}, bf16[245,1024]{1,0:T(8,128)(2,1)}, bf16[56,128,256]{2,1,0:T(8,128)(2,1)}, bf16[72,256,128]{2,1,0:T(8,128)(2,1)}, f32[16,1024]{1,0:T(8,128)}) custom-call(s32[768]{0:T(1024)} %select_reduce_fusion.block_at, bf16[49,16,128]{2,1,0:T(8,128)(2,1)} %pad_maximum_fusion.shard, bf16[245,1024]{1,0:T(8,128)(2,1)} %patches.1, ...), custom_call_target="tpu_custom_call" | custom-call | flops 12999999488 | bytes 60000000 | tf_op jit(solution)/shard_map/forward_backward/pallas_call | solution.py:475
  113.5 0.6 fusion.3
  114.1 0.0 copy-start.2
  114.2 0.0 copy-start.3
  114.2 82.2 %sum_gradients.1 = (f32[6,128,128]{2,1,0:T(8,128)}, f32[16,128]{1,0:T(8,128)}, f32[8,128]{1,0:T(8,128)}) custom-call(s32[768]{0:T(1024)} %get-tuple-element.68.left_at, s32[768]{0:T(1024)} %get-tuple-element.67.right_at, bf16[56,128,256]{2,1,0:T(8,128)(2,1)} %get-tuple-element.30.left, bf16[72,256,128]{2,1,0:T(8,128)(2,1)} %get-tuple-element.31.right, ...), custom_call_target="tpu_custom_call" | custom-call | flops 6499999744 | bytes 10000000 | tf_op jit(solution)/shard_map/sum_gradients/pallas_call | solution.py:831
  196.4 0.1 copy.30.vectors
  196.5 0.1 copy.31.vec_accum
  196.6 1.0 copy-done.5
  197.6 0.7 copy-done.6
  198.3 0.7 copy-done.7
  199.0 4.6 %update.1 = (f32[6,128,128]{2,1,0:T(8,128)}, f32[6,128,128]{2,1,0:T(8,128)}, f32[6,128,128]{2,1,0:T(8,128)}, f32[6,128,128]{2,1,0:T(8,128)}, bf16[6,128,128]{2,1...) custom-call(f32[6,128,128]{2,1,0:T(8,128)S(1)} %copy-done.5, ...), custom_call_target="tpu_custom_call" | custom-call | tf_op jit(solution)/shard_map/update/pallas_call | solution.py:912
  203.6 0.7 copy.32
  204.3 0.7 copy.33
  204.9 0.7 copy.34
  205.6 0.8 copy.38
  206.4 0.8 copy.39
  (22 shorter events, 0.0 us)
Async XLA Ops:
  6.7 106.8 %copy-start.10 = (s32[768]{0:T(1024)S(1)}, s32[768]{0:T(1024)}, u32[]{:S(2)}) copy-start(s32[768]{0:T(1024)} %param.15) | copy-start | bytes 9220
  114.1 82.3 %copy-start.11 = (f32[12,8]{0,1:T(8,128)S(1)}, f32[12,8]{0,1:T(8,128)}, u32[]{:S(2)}) copy-start(f32[12,8]{0,1:T(8,128)} %param.21) | copy-start | bytes 1156
  114.1 82.4 %copy-start.12 = (f32[12,8]{0,1:T(8,128)S(1)}, f32[12,8]{0,1:T(8,128)}, u32[]{:S(2)}) copy-start(f32[12,8]{0,1:T(8,128)} %param.22) | copy-start | bytes 1156
  114.1 82.5 %copy-start = (f32[6,128,128]{2,1,0:T(8,128)S(1)}, f32[6,128,128]{2,1,0:T(8,128)}, u32[]{:S(2)}) copy-start(f32[6,128,128]{2,1,0:T(8,128)} %master.1) | copy-start | bytes 1179652
  114.1 82.5 %copy-start.1 = (f32[6,128,128]{2,1,0:T(8,128)S(1)}, f32[6,128,128]{2,1,0:T(8,128)}, u32[]{:S(2)}) copy-start(f32[6,128,128]{2,1,0:T(8,128)} %left_stats.1) | copy-start | bytes 1179652
  114.1 82.5 %copy-start.2 = (f32[6,128,128]{2,1,0:T(8,128)S(1)}, f32[6,128,128]{2,1,0:T(8,128)}, u32[]{:S(2)}) copy-start(f32[6,128,128]{2,1,0:T(8,128)} %right_stats.1) | copy-start | bytes 1179652
  114.2 82.5 %copy-start.3 = (f32[6,128,128]{2,1,0:T(8,128)S(1)}, f32[6,128,128]{2,1,0:T(8,128)}, u32[]{:S(2)}) copy-start(f32[6,128,128]{2,1,0:T(8,128)} %left_root.1) | copy-start | bytes 1179652
  114.2 82.5 %copy-start.4 = (f32[6,128,128]{2,1,0:T(8,128)S(1)}, f32[6,128,128]{2,1,0:T(8,128)}, u32[]{:S(2)}) copy-start(f32[6,128,128]{2,1,0:T(8,128)} %right_root.1) | copy-start | bytes 1179652
  196.6 1.0 copy-start.5
  197.6 0.7 copy-start.6
  198.3 0.7 copy-start.7
  199.0 6.6 %copy-start.9 = (bf16[245,1024]{1,0:T(8,128)(2,1)S(1)}, bf16[245,1024]{1,0:T(8,128)(2,1)}, u32[]{:S(2)}) copy-start(bf16[245,1024]{1,0:T(8,128)(2,1)} %get-tuple-element.80) | copy-start | bytes 1505284
  199.0 7.4 %copy-start.8 = (bf16[245,1024]{1,0:T(8,128)(2,1)S(1)}, bf16[245,1024]{1,0:T(8,128)(2,1)}, u32[]{:S(2)}) copy-start(bf16[245,1024]{1,0:T(8,128)(2,1)} %get-tuple-element.81) | copy-start | bytes 1505284

commit v2 on v1

v2 whole, which is shorter than its diff:
```python
import functools
import math

import jax
import jax.numpy as jnp
import numpy as np
from jax import lax
from jax.experimental import pallas as pl
from jax.experimental.pallas import tpu as pltpu
from jax.sharding import PartitionSpec as P

MESH = pl.DeviceIdType.MESH
BOTH = ("wide", "narrow")
F32, BF16 = jnp.float32, jnp.bfloat16
MIB = 2**20

D = 1024
FF = 4096
HEADS = 16
HEAD_DIM = 64
PATCHES = 49
IMAGES = 5
TOKENS = IMAGES * PATCHES
ROWS = 256
SIDE = 128
NBLK = 768
NV = 12
LAYER_EPS = 1e-05
MASKED = -1000000000.0
OUTSIDE = -3.0e38
SCALE = HEAD_DIM**-0.5

ORDERS = ((0, 1, 2), (1, 2, 0), (2, 0, 1))
SHARE = (16, 16, 17)
PART_FROM = (0, 128 * 16, 128 * 32)
ALL_ROWS = 128 * 49
NEXT = (0, 3, 1, 2)

FIRST = (0, 64, 128, 192, 256, 512)
WIDTH = (8, 8, 8, 8, 32, 8)
LEFT_AT = (0, 0, 0, 8, 16, 24)
RIGHT_AT = (0, 8, 16, 24, 32, 64)


def slot_places():
    block_at, vector_at = np.zeros(NBLK, np.int32), np.zeros(128, np.int32)
    for dev in range(128):
        wide, narrow = dev // 8, dev % 8
        core = wide % 2
        pos = (wide // 2 % 2 * 2 + narrow // 4, wide // 4, narrow % 4)
        for p, (a, b, c) in enumerate(ORDERS):
            at = PART_FROM[p] + (((core * 4 + pos[c]) * 4 + pos[b]) * 4 + pos[a]) * SHARE[p]
            block_at[dev * 6 + 2 * p] = at
            block_at[dev * 6 + 2 * p + 1] = at + 8
            if p == 2:
                vector_at[dev] = at + 16
    return block_at, vector_at


BLOCK_AT, VECTOR_AT = slot_places()


def place():
    wide, narrow = lax.axis_index("wide"), lax.axis_index("narrow")
    x = (wide // 2) % 2 * 2 + narrow // 4
    return (x, wide // 4, narrow % 4), wide % 2


def device(pos, core):
    x, y, z = pos
    return ((y * 2 + x // 2) * 2 + core, x % 2 * 4 + z)


def moved(pos, axis, by):
    return tuple((c + by) % 4 if a == axis else c for a, c in enumerate(pos))


def partners():
    pos, core = place()
    plane = [device(moved(moved(pos, 0, i), 1, j), core) for i in range(4) for j in range(4) if i or j]
    column = [
        device(moved(pos, 2, i), core if j == 0 else 1 - core) for j in range(2) for i in range(4) if i or j
    ]
    return plane, column


def announce(semaphore):
    plane, column = partners()
    for partner in plane + column:
        pl.semaphore_signal(semaphore, inc=1, device_id=partner, device_id_type=MESH)


def all_announced(semaphore):
    plane, column = partners()
    pl.semaphore_wait(semaphore, len(plane + column))


def loop(count, body):
    lax.fori_loop(0, count, lambda i, _: (body(i), None)[1], None)


def dot(left, right):
    return jnp.dot(left, right, preferred_element_type=F32)


def dot_nt(left, right):
    return lax.dot_general(left, right, (((1,), (1,)), ((), ())), preferred_element_type=F32)


def dot_tn(left, right):
    return lax.dot_general(left, right, (((0,), (0,)), ((), ())), preferred_element_type=F32)


def gather_weights(master, vectors, loads, g, send_sem, recv_sem, meanwhile):
    pos, core = place()
    twin = device(pos, 1 - core)
    near = {(a, s): device(moved(pos, a, s), core) for a in range(3) for s in (1, -1)}

    for load in loads:
        load.wait()

    for p in range(3):
        a, b, c = (pos[axis] for axis in ORDERS[p])
        start = PART_FROM[p] + (((core * 4 + c) * 4 + b) * 4 + a) * SHARE[p]
        g[pl.ds(start, 16)] = master[2 * p : 2 * p + 2].astype(BF16).reshape(16, 16, SIDE)
        if p == 2:
            wide, narrow = lax.axis_index("wide"), lax.axis_index("narrow")
            first_lane = (lax.rem(wide, 2) * 8 + narrow) * 8
            spread = lax.broadcasted_iota(jnp.int32, (8, 128), 1) == (
                lax.broadcasted_iota(jnp.int32, (8, 128), 0) + first_lane
            )
            tile = dot_tn(vectors[...].astype(BF16), spread.astype(BF16)).astype(BF16)
            g[start + 16] = jnp.concatenate([tile, jnp.zeros((16 - NV, 128), BF16)], 0)

    sends = []

    def copy_of(src, dst, p, slot, to):
        return pltpu.make_async_remote_copy(
            src_ref=src, dst_ref=dst, send_sem=send_sem.at[p, slot],
            recv_sem=recv_sem.at[p, slot], device_id=to, device_id_type=MESH,
        )

    def send(src, dst, p, slot, to):
        copy = copy_of(src, dst, p, slot, to)
        copy.start()
        sends.append(copy)

    def arrived(dst, p, slot):
        copy_of(dst, dst, p, slot, twin).wait_recv()

    def at(p, of_core, c, b, a=0, count=4, skip=0, rows=None):
        start = PART_FROM[p] + (((of_core * 4 + c % 4) * 4 + b % 4) * 4 + a % 4) * SHARE[p] + skip
        return g.at[pl.ds(start, count * SHARE[p] if rows is None else rows)]

    def spot(p):
        a, b, c = ORDERS[p]
        return pos[a], pos[b], pos[c]

    def row(p, ci, bi):
        _, b, c = spot(p)
        return at(p, core, c + ci, b + bi)

    def half_row(p, ci, bi, second):
        _, b, c = spot(p)
        return at(p, core, c + ci, b + bi, 2 if second else 0, 2)

    def chunk(p, ai):
        a, b, c = spot(p)
        return at(p, core, c, b, a + ai, 1)

    def half_chunk(p, ai, second):
        a, b, c = spot(p)
        return at(p, core, c, b, a + ai, 1, 8 if second else 0, SHARE[p] - 8 if second else 8)

    def to_twin(p, ci, bi):
        r = row(p, ci, bi)
        send(r, r, p, 24 + 4 * (ci % 4) + bi % 4, twin)

    def onward(p, base, axis, half):
        first, second = half(False), half(True)
        return (
            lambda: send(first, first, p, base + 2, near[axis, 1]),
            lambda: send(second, second, p, base + 3, near[axis, -1]),
        )

    def both(p, base, axis, src, dst):
        send(src, dst, p, base, near[axis, 1])
        send(src, dst, p, base + 1, near[axis, -1])

    parts = range(3)
    for p in parts:
        both(p, 0, ORDERS[p][0], chunk(p, 0), chunk(p, 0))
    for p in parts:
        axis = ORDERS[p][0]
        arrived(chunk(p, -1), p, 0)
        onward(p, 0, axis, lambda second: half_chunk(p, -1, second))[0]()
        arrived(chunk(p, 1), p, 1)
        onward(p, 0, axis, lambda second: half_chunk(p, 1, second))[1]()
    for p in parts:
        arrived(half_chunk(p, 2, False), p, 2)
        arrived(half_chunk(p, 2, True), p, 3)
        r = row(p, 0, 0)
        both(p, 4, ORDERS[p][1], r, r)
        both(p, 8, ORDERS[p][2], r, r)
        to_twin(p, 0, 0)
    for p in parts:
        for bi, i in ((-1, 1), (1, 2)):
            r = row(p, 0, bi)
            arrived(r, p, 4 + (i - 1))
            onward(p, 4, ORDERS[p][1], lambda second: half_row(p, 0, bi, second))[i - 1]()
            both(p, 8 + 4 * i, ORDERS[p][2], r, r)
            to_twin(p, 0, bi)

    meanwhile()

    def sides(p, i):
        bi = NEXT[i]
        for ci, j in ((-1, 0), (1, 1)):
            arrived(row(p, ci, bi), p, 8 + 4 * i + j)
            onward(p, 8 + 4 * i, ORDERS[p][2], lambda second: half_row(p, ci, bi, second))[j]()
            to_twin(p, ci, bi)

    def opposite(p, i):
        bi = NEXT[i]
        arrived(half_row(p, 2, bi, False), p, 8 + 4 * i + 2)
        arrived(half_row(p, 2, bi, True), p, 8 + 4 * i + 3)
        to_twin(p, 2, bi)

    for p in parts:
        sides(p, 0)
    for p in parts:
        arrived(half_row(p, 0, 2, False), p, 6)
        arrived(half_row(p, 0, 2, True), p, 7)
        r = row(p, 0, 2)
        both(p, 8 + 12, ORDERS[p][2], r, r)
        to_twin(p, 0, 2)
    for p in parts:
        sides(p, 1)
        sides(p, 2)
    for p in parts:
        opposite(p, 0)
    for p in parts:
        sides(p, 3)
    for p in parts:
        opposite(p, 1)
        opposite(p, 2)
    for p in parts:
        opposite(p, 3)
    for p in parts:
        _, b, c = spot(p)
        for ci in range(4):
            for bi in range(4):
                arrived(at(p, 1 - core, c + ci, b + bi), p, 24 + 4 * ci + bi)
    return sends


def normal(values):
    centre = jnp.mean(values, -1, keepdims=True)
    centred = values - centre
    spread = jnp.mean(centred * centred, -1, keepdims=True)
    scale = lax.rsqrt(spread + LAYER_EPS)
    return centred * scale, scale


def by_eights(values):
    return jnp.sum(values.reshape(values.shape[0] // 8, 8, values.shape[1]), 0)


def pass_kernel(
    block_at, master_in, vectors_in, patches, keep_in, cotangent, output, input_grad, vec_out,
    g, left, right, flats, q, k, v, att, a_low, probs, act, w_out, wall, sums, vec,
    master, vectors, keep, send_sem, recv_sem, held_sem, ready,
):
    tokens, d_mid, mid, d_a = (flats.at[i] for i in range(4))
    loads = [
        pltpu.make_async_copy(src, to, held_sem.at[i])
        for i, (src, to) in enumerate(
            ((master_in, master), (vectors_in, vectors), (patches, output), (cotangent, input_grad), (keep_in, keep))
        )
    ]
    for load in loads:
        load.start()

    def block(n):
        return g[pl.ds(block_at[n], 8)].reshape(SIDE, SIDE)

    def columns(m, j, count):
        rows = (256 if m == 4 else 64 if m < 4 else 256) // WIDTH[m]
        return jnp.concatenate(
            [
                jnp.concatenate([block(FIRST[m] + r * WIDTH[m] + j + i) for i in range(count)], 1)
                for r in range(rows)
            ],
            0,
        )

    def rows_of(m, i, count):
        return jnp.concatenate(
            [
                jnp.concatenate([block(FIRST[m] + (i + r) * WIDTH[m] + c) for c in range(WIDTH[m])], 1)
                for r in range(count)
            ],
            0,
        )

    def lanes(i, width):
        return pl.ds(pl.multiple_of(i * width, width), width)

    def strip(i):
        return pl.ds(pl.multiple_of(i * 32, 32), 32)

    def stack(first, count):
        return jnp.concatenate([right[first + i] for i in range(count)], 1)

    def line(i):
        return vec[i : i + 1, :]

    def add_sums(i, value, where=slice(None)):
        sums[i, :, where] += by_eights(value)

    def first_normal(i):
        n, _ = normal(tokens[strip(i), :])
        d_a[strip(i), :] = n
        cot = d_mid[strip(i), :]
        for c in range(8):
            right[64 + c, strip(i), :] = cot[:, c * 128 : (c + 1) * 128].astype(BF16)
        add_sums(7, cot)

    def meanwhile():
        sums[...] = jnp.zeros_like(sums)
        for load in loads[2:]:
            load.wait()
        for came, to in ((output, tokens), (input_grad, d_mid)):
            to[0:TOKENS, :] = came[...].astype(F32)
            to[TOKENS:ROWS, :] = jnp.zeros((ROWS - TOKENS, D), F32)
        row_at = lax.broadcasted_iota(jnp.int32, (ROWS, ROWS), 0)
        col_at = lax.broadcasted_iota(jnp.int32, (ROWS, ROWS), 1)

        def image(at):
            return sum((at >= PATCHES * (i + 1)).astype(jnp.int32) for i in range(IMAGES))

        spread = (
            lax.broadcasted_iota(jnp.int32, (PATCHES, ROWS), 1)
            - PATCHES * image(lax.broadcasted_iota(jnp.int32, (PATCHES, ROWS), 1))
            == lax.broadcasted_iota(jnp.int32, (PATCHES, ROWS), 0)
        )
        kept = dot(keep[...].astype(F32).astype(BF16), spread.astype(F32).astype(BF16))
        own = lax.broadcasted_iota(jnp.int32, (IMAGES, ROWS), 0) == image(
            lax.broadcasted_iota(jnp.int32, (IMAGES, ROWS), 1)
        )
        dropped = jnp.sum(jnp.where(own & (kept < 0.5), 1.0, 0.0), 0, keepdims=True)
        wall[...] = jnp.where(
            image(row_at) == image(col_at), jnp.broadcast_to(dropped, (ROWS, ROWS)) * MASKED, OUTSIDE
        )
        loop(8, first_normal)

    barrier = pltpu.get_barrier_semaphore()
    announce(barrier)
    all_announced(barrier)
    sends = gather_weights(master, vectors, loads[:2], g, send_sem, recv_sem, meanwhile)

    for w in range(8):
        window = sum(g[int(VECTOR_AT[16 * w + i])].astype(F32) for i in range(16))
        vec[:, w * 128 : (w + 1) * 128] = window

    def first_norm(i):
        a_low[strip(i), :] = (d_a[strip(i), :] * line(0) + line(1)).astype(BF16)

    loop(8, first_norm)

    def project(j):
        left[pl.ds(2 * j, 2)] = a_low[:, lanes(j, 256)].T.reshape(2, 128, ROWS)
        at = lanes(j, 256)
        q[:, at] = (dot(a_low[...], columns(0, 2 * j, 2)) + vec[2:3, at]).astype(BF16)
        k[:, at] = dot(a_low[...], columns(1, 2 * j, 2)).astype(BF16)
        v[:, at] = (dot(a_low[...], columns(2, 2 * j, 2)) + vec[3:4, at]).astype(BF16)

    loop(4, project)

    low_half = lax.broadcasted_iota(jnp.int32, (ROWS, 128), 1) < HEAD_DIM

    def split(pair):
        nothing = jnp.zeros_like(pair)
        return jnp.where(low_half, pair, nothing), jnp.where(low_half, nothing, pair)

    def attend(j):
        at = lanes(j, 128)
        kp = k[:, at]
        weights = []
        for h, qh in enumerate(split(q[:, at])):
            raw = dot_nt(qh, kp)
            masked = jnp.where(wall[...] == 0.0, raw * SCALE, wall[...])
            e = jnp.exp(masked - jnp.max(masked, -1, keepdims=True))
            p = e / jnp.sum(e, -1, keepdims=True)
            low = p.astype(BF16)
            probs[2 * j + h] = low
            weights.append(low)
        pair = dot(jnp.concatenate(weights, 1), jnp.concatenate(split(v[:, at]), 0)).astype(BF16)
        att[:, at] = pair
        left[8 + j] = pair.T

    loop(8, attend)

    def to_mid(j):
        at = lanes(j, 256)
        mid[:, at] = tokens[:, at] + (dot(att[...], columns(3, 2 * j, 2)) + vec[4:5, at])

    loop(4, to_mid)

    def second_norm(i):
        n, _ = normal(mid[strip(i), :])
        a_low[strip(i), :] = (n * line(5) + line(6)).astype(BF16)

    loop(8, second_norm)

    def hidden(j):
        pre = dot(a_low[...], columns(4, 2 * j, 2)) + vec[pl.ds(8 + j // 4, 1), lanes(j % 4, 256)]
        half = 0.5 * (1.0 + lax.erf(pre * math.sqrt(0.5)))
        slope = half + pre * (jnp.exp(-0.5 * pre * pre) * (1.0 / math.sqrt(2.0 * math.pi)))
        low = (pre * half).astype(BF16)
        act[:, lanes(j, 256)] = low
        left[pl.ds(24 + 2 * j, 2)] = low.T.reshape(2, 128, ROWS)
        weights = rows_of(5, 2 * j, 2)
        w_out[lanes(j, 256), :] = weights
        d_pre = (dot_nt(stack(64, 8), weights) * slope).astype(BF16)
        right[32 + 2 * j] = d_pre[:, :128]
        right[33 + 2 * j] = d_pre[:, 128:]
        add_sums(8 + j // 4, d_pre.astype(F32), lanes(j % 4, 256))

    loop(16, hidden)

    def second_back(j):
        at = lanes(j, 256)
        left[pl.ds(16 + 2 * j, 2)] = a_low[:, at].T.reshape(2, 128, ROWS)
        d_a[:, at] = dot_nt(stack(32, 32), rows_of(4, 2 * j, 2))

    loop(4, second_back)

    def mid_back(i):
        rows = strip(i)
        n, scale = normal(mid[rows, :])
        d = d_a[rows, :]
        e = d * line(5)
        inner = e - jnp.mean(e, -1, keepdims=True) - n * jnp.mean(e * n, -1, keepdims=True)
        whole = d_mid[rows, :] + inner * scale
        d_mid[rows, :] = whole
        low = whole.astype(BF16)
        for c in range(8):
            right[24 + c, rows, :] = low[:, c * 128 : (c + 1) * 128]
        add_sums(5, d * n)
        add_sums(6, d)
        add_sums(4, low.astype(F32))

    loop(8, mid_back)

    def att_back(j):
        att[:, lanes(j, 256)] = dot_nt(stack(24, 8), rows_of(3, 2 * j, 2)).astype(BF16)

    loop(4, att_back)

    def heads_back(j):
        at = lanes(j, 128)
        vp = v[:, at]
        q_parts, k_parts, da_parts = split(q[:, at]), split(k[:, at]), split(att[:, at])
        d_raws, weights = [], []
        for h in range(2):
            low = probs[2 * j + h]
            p = low.astype(F32)
            d_p = dot_nt(da_parts[h], vp)
            d_m = p * (d_p - jnp.sum(p * d_p, -1, keepdims=True))
            d_raws.append(jnp.where(wall[...] == 0.0, d_m * SCALE, 0.0).astype(BF16))
            weights.append(low)
        d_q = dot(jnp.concatenate(d_raws, 1), jnp.concatenate(k_parts, 0)).astype(BF16)
        d_k = dot_tn(jnp.concatenate(d_raws, 0), jnp.concatenate(q_parts, 0)).astype(BF16)
        d_v = dot_tn(jnp.concatenate(weights, 0), jnp.concatenate(da_parts, 0)).astype(BF16)
        right[j] = d_q
        right[8 + j] = d_k
        right[16 + j] = d_v
        add_sums(2, d_q.astype(F32), at)
        add_sums(3, d_v.astype(F32), at)

    loop(8, heads_back)

    def first_back(j):
        weights = jnp.concatenate([rows_of(m, 2 * j, 2) for m in range(3)], 1)
        d_a[:, lanes(j, 256)] = dot_nt(stack(0, 24), weights)

    loop(4, first_back)

    def token_back(i):
        rows = strip(i)
        n, scale = normal(tokens[rows, :])
        d = d_a[rows, :]
        e = d * line(0)
        inner = e - jnp.mean(e, -1, keepdims=True) - n * jnp.mean(e * n, -1, keepdims=True)
        d_mid[rows, :] = d_mid[rows, :] + inner * scale
        add_sums(0, d * n)
        add_sums(1, d)

    for copy in sends:
        copy.wait_send()
    announce(ready)
    loop(8, token_back)
    input_grad[...] = d_mid[0:TOKENS, :].astype(BF16)
    folded = jnp.sum(sums[...], 1)
    vec_out[0] = folded[:8]
    vec_out[1, 0 : NV - 8] = folded[8:]
    vec_out[1, NV - 8 :] = jnp.zeros((16 - NV, D), F32)

    def last(j):
        at = lanes(j, 256)
        d_a[:, at] = mid[:, at] + (dot(act[...], w_out[:, at]) + vec[7:8, at])

    return last


ROUNDS = (
    (2, 2), (2, 1), (1, 2), (3, 2), (2, 3), (1, 1), (3, 1), (0, 2), (2, 0), (1, 3), (3, 3), (0, 1), (1, 0), (3, 0), (0, 3), (0, 0),
)
AHEAD = 1
RING = 2 * AHEAD + 2


VMEM_LIMIT = 62 * MIB


class Rows:
    def __init__(self, buffer, first):
        self.buffer, self.first = buffer, first

    def row(self, n):
        return self.buffer.at[pl.ds(64 * (self.first + n), 64)]

    def half(self, n, second):
        return self.buffer.at[pl.ds(64 * (self.first + n) + 32 * second, 32)]

    def get(self, n, ai):
        return self.buffer[pl.ds(64 * (self.first + n) + 16 * ai, 16)].reshape(256, SIDE).astype(F32)

    def put(self, n, ai, value):
        self.buffer[pl.ds(64 * (self.first + n) + 16 * ai, 16)] = value.astype(BF16).reshape(16, 16, SIDE)


def scatter_kernel(
    left_at, right_at, left, right, vec_in,
    total, window, norm_tile,
    g, kept, b_out, b_in, b_half, a_out, a_in,
    vec_y, vec_y_in, vec_x, vec_x_in, vec_z, vec_z_in, vec_t, tiles,
    tw_send, tw_recv, c_send, c_recv, b_send, b_recv, a_send, a_recv, v_send, v_recv, n_send, n_recv,
    between,
):
    pos, core = place()
    twin = device(pos, 1 - core)
    axes = [[device(moved(pos, a, s), core) for s in (1, 2, 3)] for a in range(3)]
    plane, column = partners()
    tw_out, tw_in, c_out, c_in, c_half = (Rows(g, at) for at in (0, 3 * RING, 6 * RING, 6 * RING + 36, 6 * RING + 60))

    def pick(options, i):
        value = options[-1]
        for n in range(len(options) - 2, -1, -1):
            value = jnp.where(i == n, options[n], value)
        return value

    def axis_of(p, which):
        return lax.rem(p + which, 3)

    def neighbour(p, which, by):
        axis = axis_of(p, which)
        return tuple(pick([axes[a][by - 1][n] for a in range(3)], axis) for n in range(2))

    def along(p, which, by):
        return lax.rem(pick(pos, axis_of(p, which)) + by, 4)

    def pair(p, ci, bi, ai, of_core):
        spots = [along(p, 0, ai), along(p, 1, bi), along(p, 2, ci)]
        x, y, z = (pick([spots[(a - s) % 3] for s in range(3)], p) for a in range(3))
        wide, narrow = device((x, y, z), of_core)
        slot = (wide * 8 + narrow) * 6 + 2 * p
        made = []
        for i in range(2):
            made.append(dot(left[left_at[slot + i]], right[right_at[slot + i]]))
        return jnp.concatenate(made, 0)

    def remote(src, dst, send_sem, recv_sem, to):
        return pltpu.make_async_remote_copy(
            src_ref=src, dst_ref=dst, send_sem=send_sem, recv_sem=recv_sem, device_id=to, device_id_type=MESH
        )

    def twin_copy(k, p):
        n = 3 * (k % RING) + p
        return remote(tw_out.row(n), tw_in.row(n), tw_send.at[3 * k + p], tw_recv.at[3 * k + p], twin)

    def for_twin(k, p):
        if k >= len(ROUNDS):
            return
        if k >= RING:
            twin_copy(k - RING, p).wait_send()
        ci, bi = ROUNDS[k]
        for ai in range(4):
            tw_out.put(3 * (k % RING) + p, ai, pair(p, ci, bi, ai, 1 - core))
        twin_copy(k, p).start()

    def chip_sum(k, p, ai):
        ci, bi = ROUNDS[k]
        return pair(p, ci, bi, ai, core) + tw_in.get(3 * (k % RING) + p, ai)

    def c_half_copy(p, bi, second):
        n = p * 4 + bi
        return remote(
            c_out.half(n, second), c_half.half(n, second), c_send.at[2 * n + second], c_recv.at[2 * n + second],
            neighbour(p, 2, 3 if second else 1),
        )

    def c_whole_copy(p, bi, leftward):
        n = 12 * leftward + p * 4 + bi
        return remote(
            c_out.row(12 + n), c_in.row(n), c_send.at[24 + n], c_recv.at[24 + n], neighbour(p, 2, 3 if leftward else 1)
        )

    def b_half_copy(p, second):
        part = pl.ds(2 * second, 2)
        return remote(
            b_out.at[p, 0, part], b_half.at[p, part], b_send.at[4 * p + second], b_recv.at[4 * p + second],
            neighbour(p, 1, 3 if second else 1),
        )

    def b_whole_copy(p, leftward):
        return remote(
            b_out.at[p, 1 + leftward], b_in.at[p, leftward], b_send.at[4 * p + 2 + leftward],
            b_recv.at[4 * p + 2 + leftward], neighbour(p, 1, 3 if leftward else 1),
        )

    def a_copy(p, by):
        n = 3 * p + by - 1
        return remote(a_out.at[n], a_in.at[n], a_send.at[n], a_recv.at[n], neighbour(p, 0, by))

    def opposite_row(k, p):
        _, bi = ROUNDS[k]
        for ai in range(4):
            c_out.put(p * 4 + bi, ai, chip_sum(k, p, ai))
            if ai % 2:
                c_half_copy(p, bi, ai // 2).start()

    def side_row(k, p):
        ci, bi = ROUNDS[k]
        leftward = ci // 2
        n = p * 4 + bi
        c_half_copy(p, bi, leftward).wait_recv()
        for ai in range(4):
            value = chip_sum(k, p, ai)
            if ai // 2 == leftward:
                value = value + c_half.get(n, ai)
            c_out.put(12 + 12 * leftward + n, ai, value)
        c_whole_copy(p, bi, leftward).start()

    def own_row(k, p):
        _, bi = ROUNDS[k]
        n = p * 4 + bi
        leftward = bi // 2
        c_whole_copy(p, bi, 0).wait_recv()
        c_whole_copy(p, bi, 1).wait_recv()
        if bi % 2:
            b_half_copy(p, leftward).wait_recv()
        for ai in range(4):
            value = chip_sum(k, p, ai) + c_in.get(n, ai) + c_in.get(12 + n, ai)
            if bi == 0:
                kept[p, :, ai * 128 : (ai + 1) * 128] = value
                continue
            if bi % 2 and ai // 2 == leftward:
                value = value + b_half[p, ai].astype(F32)
            b_out[p, 0 if bi == 2 else 1 + leftward, ai] = value.astype(BF16)
            if bi == 2 and ai % 2:
                b_half_copy(p, ai // 2).start()
        if bi % 2:
            b_whole_copy(p, leftward).start()

    def vec_twin():
        return remote(vec_in.at[1 - core], vec_t.at[0], v_send.at[0], v_recv.at[0], twin)

    def vec_copy(axis, by):
        src, dst = ((vec_x, vec_x_in), (vec_y, vec_y_in), (vec_z, vec_z_in))[axis]
        n = 1 + 3 * axis + by - 1
        there = lax.rem(pos[axis] + by, 4)
        piece = src.at[there] if axis == 1 else src.at[there // 2] if axis == 0 else src
        return remote(piece, dst.at[by - 1], v_send.at[n], v_recv.at[n], axes[axis][by - 1])

    def vec_start(axis):
        for by in (1, 2, 3):
            vec_copy(axis, by).start()

    def vec_sum(axis, whole):
        dst = (vec_x_in, vec_y_in, vec_z_in)[axis]
        for by in (1, 2, 3):
            vec_copy(axis, by).wait_recv()
            whole = whole + dst[by - 1]
        return whole

    def vec_last():
        return remote(window.at[core], window.at[core], v_send.at[10], v_recv.at[10], twin)

    def vec_stage(stage):
        if stage == 0:
            vec_twin().wait_recv()
            whole = vec_in[core] + vec_t[0]
            for i in range(4):
                vec_y[i] = whole[:, 256 * i : 256 * i + 256]
            vec_start(1)
        elif stage == 1:
            whole = vec_sum(1, vec_y[pos[1]])
            for i in range(2):
                vec_x[i] = whole[:, 128 * i : 128 * i + 128]
            vec_start(0)
        elif stage == 2:
            vec_z[...] = vec_sum(0, vec_x[pos[0] // 2])
            vec_start(2)
        elif stage == 3:
            window[core] = vec_sum(2, vec_z[...])
            vec_last().start()

    vec_twin().start()
    for k in range(AHEAD):
        loop(3, lambda p: for_twin(k, p))
    for k, (ci, _) in enumerate(ROUNDS):

        def one_round(p):
            for_twin(k + AHEAD, p)
            twin_copy(k, p).wait_recv()
            (own_row if ci == 0 else opposite_row if ci == 2 else side_row)(k, p)

        loop(3, one_round)
        if k % 3 == 2:
            vec_stage(k // 3)
        between(k)

    def row_sum(p, ai):
        return kept[p, :, ai * 128 : (ai + 1) * 128] + b_in[p, 0, ai].astype(F32) + b_in[p, 1, ai].astype(F32)

    def last_axis(p):
        b_whole_copy(p, 0).wait_recv()
        b_whole_copy(p, 1).wait_recv()
        for by in (2, 1, 3):
            a_out[3 * p + by - 1] = row_sum(p, by).astype(BF16)
            a_copy(p, by).start()

    loop(3, last_axis)

    wide, narrow = lax.axis_index("wide"), lax.axis_index("narrow")
    remote(window.at[1 - core], window.at[1 - core], v_send.at[10], v_recv.at[10], twin).wait_recv()
    lane = lax.broadcasted_iota(jnp.int32, (8, 128), 1) // 8
    own_lanes = lane == lax.rem(wide, 2) * 8 + narrow
    squares = jnp.zeros((8, 128), F32)
    for i in range(2):
        own = jnp.where(own_lanes, window[i], 0.0)
        squares = squares + own * own

    for p in range(3):
        value = row_sum(p, 0)
        for by in (1, 3, 2):
            a_copy(p, by).wait_recv()
            value = value + a_in[3 * p + by - 1].astype(F32)
        total[2 * p] = value[:128]
        total[2 * p + 1] = value[128:]
        squares = squares + by_eights(value * value)

    def norm_copy(stage, i):
        n = 15 * stage + i
        to = (column if stage else plane)[i]
        return remote(tiles.at[stage], tiles.at[2 + n], n_send.at[n], n_recv.at[n], to)

    whole = squares
    for stage, count in ((0, 15), (1, 7)):
        tiles[stage] = whole
        for i in range(count):
            norm_copy(stage, i).start()
        for i in range(count):
            norm_copy(stage, i).wait_recv()
            whole = whole + tiles[2 + 15 * stage + i]
    norm_tile[...] = whole

    def sent(p):
        for k in range(len(ROUNDS) - RING, len(ROUNDS)):
            twin_copy(k, p).wait_send()
        for side in (0, 1):
            for bi in range(4):
                c_half_copy(p, bi, side).wait_send()
                c_whole_copy(p, bi, side).wait_send()
            b_half_copy(p, side).wait_send()
            b_whole_copy(p, side).wait_send()
        for by in (1, 2, 3):
            a_copy(p, by).wait_send()

    loop(3, sent)
    vec_twin().wait_send()
    vec_last().wait_send()
    for axis in range(3):
        for by in (1, 2, 3):
            vec_copy(axis, by).wait_send()
    for stage, count in ((0, 15), (1, 7)):
        for i in range(count):
            norm_copy(stage, i).wait_send()


def whole_kernel(
    block_at, left_at, right_at, master_in, vectors_in, patches, keep_in, cotangent,
    output, input_grad, total, window, norm_tile, *scratch,
):
    gathered, scattered = scratch[:PASS_SCRATCH], scratch[PASS_SCRATCH:]
    g, left, right, flats = gathered[:4]
    vec_in, *scattered = scattered
    ready = gathered[-1]
    last = pass_kernel(
        block_at, master_in, vectors_in, patches, keep_in, cotangent, output, input_grad, vec_in, *gathered
    )
    all_announced(ready)

    def between(k):
        if 1 <= k <= 4:
            last(k - 1)

    scatter_kernel(left_at, right_at, left, right, vec_in, total, window, norm_tile, g, flats, *scattered, between)
    output[...] = flats[3, 0:TOKENS, :].astype(BF16)


PASS_SCRATCH = 22


def forward_backward(block_at, left_at, right_at, master, vectors, patches, keep, cotangent):
    vmem = pl.BlockSpec(memory_space=pltpu.VMEM)
    flat, row = (ROWS, D), (4, 256, 128)
    dma = pltpu.SemaphoreType.DMA
    pass_scratch = [
        pltpu.VMEM((ALL_ROWS, 16, 128), BF16),
        pltpu.VMEM((56, 128, ROWS), BF16),
        pltpu.VMEM((72, ROWS, 128), BF16),
        pltpu.VMEM((4, *flat), F32),
        *[pltpu.VMEM(flat, BF16)] * 5,
        pltpu.VMEM((HEADS, ROWS, ROWS), BF16),
        pltpu.VMEM((ROWS, FF), BF16),
        pltpu.VMEM((FF, D), BF16),
        pltpu.VMEM((ROWS, ROWS), F32),
        pltpu.VMEM((NV, 8, D), F32),
        pltpu.VMEM((16, D), F32),
        pltpu.VMEM((6, SIDE, SIDE), F32),
        pltpu.VMEM((8, NV), F32),
        pltpu.VMEM((IMAGES, PATCHES), jnp.int32),
        dma((3, 40)),
        dma((3, 40)),
        dma((5,)),
        pltpu.SemaphoreType.REGULAR,
    ]
    assert len(pass_scratch) == PASS_SCRATCH
    return pl.pallas_call(
        whole_kernel,
        out_shape=[
            jax.ShapeDtypeStruct((TOKENS, D), BF16),
            jax.ShapeDtypeStruct((TOKENS, D), BF16),
            jax.ShapeDtypeStruct((6, SIDE, SIDE), F32),
            jax.ShapeDtypeStruct((2, 8, 128), F32),
            jax.ShapeDtypeStruct((8, 128), F32),
        ],
        in_specs=[pl.BlockSpec(memory_space=pltpu.SMEM)] * 3 + [pl.BlockSpec(memory_space=pltpu.HBM)] * 5,
        out_specs=[vmem] * 5,
        scratch_shapes=pass_scratch
        + [
            pltpu.VMEM((2, 8, D), F32),
            pltpu.VMEM((3, 3, *row), BF16),
            pltpu.VMEM((3, 2, *row), BF16),
            pltpu.VMEM((3, *row), BF16),
            pltpu.VMEM((9, 256, 128), BF16),
            pltpu.VMEM((9, 256, 128), BF16),
            pltpu.VMEM((4, 8, 256), F32),
            pltpu.VMEM((3, 8, 256), F32),
            pltpu.VMEM((2, 8, 128), F32),
            pltpu.VMEM((3, 8, 128), F32),
            pltpu.VMEM((8, 128), F32),
            pltpu.VMEM((3, 8, 128), F32),
            pltpu.VMEM((1, 8, D), F32),
            pltpu.VMEM((24, 8, 128), F32),
            dma((48,)), dma((48,)), dma((48,)), dma((48,)), dma((12,)), dma((12,)), dma((9,)), dma((9,)),
            dma((11,)), dma((11,)), dma((22,)), dma((22,)),
        ],
        compiler_params=pltpu.CompilerParams(
            collective_id=0, has_side_effects=True, vmem_limit_bytes=VMEM_LIMIT
        ),
        cost_estimate=pl.CostEstimate(
            flops=19_000_000_000, bytes_accessed=10_000_000, transcendentals=3_000_000
        ),
        name="forward_backward",
    )(block_at, left_at, right_at, master, vectors, patches, keep, cotangent)


def rounded_dot(left, right, over):
    return lax.dot_general(
        left.astype(BF16), right.astype(BF16), (over, ((), ())), preferred_element_type=F32
    )


def step_kernel(
    raw, window, norm_tile, shift, master, left_stats, right_stats, left_root, right_root, vectors, vec_accum,
    output_in, input_grad_in,
    block_grads, new_left, new_right, new_master, new_copy, vec_grads, vec_accum_new, vec_new, grad_norm,
    output, input_grad, sem,
):
    def copies():
        pairs = ((output_in, output), (input_grad_in, input_grad))
        return [pltpu.make_async_copy(src, dst, sem.at[i]) for i, (src, dst) in enumerate(pairs)]

    norm = jnp.sqrt(jnp.sum(norm_tile[...], keepdims=True))
    clip = 1.0 / jnp.maximum(norm, 1.0)

    @pl.when(pl.program_id(0) == 0)
    def _():
        for copy in copies():
            copy.start()
        grad_norm[...] = norm
        lanes = pltpu.roll(window[...].reshape(16, 128), shift[0], 1)
        grads = clip * lanes.T[:8, :NV]
        vec_grads[...] = grads
        accum = 0.5 * vec_accum[...] + 0.5 * grads * grads
        vec_accum_new[...] = accum
        vec_new[...] = vectors[...] - 0.5 * grads / (jnp.sqrt(accum) + 1e-08)

    for i in range(raw.shape[0]):
        grads = raw[i] * clip
        block_grads[i] = grads
        new_left[i] = 0.5 * left_stats[i] + 0.5 * rounded_dot(grads, grads, ((1,), (1,)))
        new_right[i] = 0.5 * right_stats[i] + 0.5 * rounded_dot(grads, grads, ((0,), (0,)))
        way = rounded_dot(rounded_dot(left_root[i], grads, ((1,), (0,))), right_root[i], ((1,), (0,)))
        master_now = master[i] - 0.5 * way
        new_master[i] = master_now
        new_copy[i] = master_now.astype(BF16)

    @pl.when(pl.program_id(0) == pl.num_programs(0) - 1)
    def _():
        for copy in copies():
            copy.wait()


def update(raw, window, norm_tile, shift, blocks_in, vectors, vec_accum, output, input_grad):
    per = 2
    blocks = pl.BlockSpec((per, SIDE, SIDE), lambda i: (i, 0, 0))
    anywhere = pl.BlockSpec(memory_space=pl.ANY)

    def whole(*shape):
        return pl.BlockSpec(shape, lambda i: (0,) * len(shape))

    f32_blocks = jax.ShapeDtypeStruct((6, SIDE, SIDE), F32)
    f32_vecs = jax.ShapeDtypeStruct((8, NV), F32)
    tokens = jax.ShapeDtypeStruct((TOKENS, D), BF16)
    return pl.pallas_call(
        step_kernel,
        grid=(6 // per,),
        out_shape=[f32_blocks] * 4
        + [jax.ShapeDtypeStruct((6, SIDE, SIDE), BF16)]
        + [f32_vecs] * 3
        + [jax.ShapeDtypeStruct((1, 1), F32)]
        + [tokens] * 2,
        in_specs=[blocks, whole(2, 8, 128), whole(8, 128), pl.BlockSpec(memory_space=pltpu.SMEM)]
        + [blocks] * 5
        + [whole(8, NV)] * 2
        + [anywhere] * 2,
        out_specs=[blocks] * 5 + [whole(8, NV)] * 3 + [whole(1, 1)] + [anywhere] * 2,
        scratch_shapes=[pltpu.SemaphoreType.DMA((2,))],
        compiler_params=pltpu.CompilerParams(vmem_limit_bytes=32 * MIB),
        name="update",
    )(raw, window, norm_tile, shift, *blocks_in, vectors, vec_accum, output, input_grad)


def body(
    patches, keep, cotangent, owner_table, master, left_stats, right_stats, left_root, right_root, vectors, vec_accum,
):
    wide, narrow = lax.axis_index("wide"), lax.axis_index("narrow")
    numbers = jnp.arange(NBLK, dtype=jnp.int32)
    held = owner_table[None, :] == numbers[:, None]
    block_at = jnp.sum(jnp.where(held, jnp.asarray(BLOCK_AT)[None, :], 0), 1)
    matrix = sum((owner_table >= first).astype(jnp.int32) for first in FIRST[1:])

    def by_matrix(values):
        return sum(jnp.where(matrix == m, value, 0) for m, value in enumerate(values))

    inner = owner_table - by_matrix(FIRST)
    block_row = jnp.where(matrix == 4, inner // 32, inner // 8)
    block_column = jnp.where(matrix == 4, inner % 32, inner % 8)
    left_at = by_matrix(LEFT_AT) + block_row
    right_at = by_matrix(RIGHT_AT) + block_column

    output, input_grad, raw, window, norm_tile = forward_backward(
        block_at, left_at, right_at, master, vectors.T, patches, keep, cotangent
    )
    lane = ((wide % 2) * 8 + narrow) * 8
    shift = jnp.reshape((128 - lane) % 128, (1,)).astype(jnp.int32)
    blocks_in = (master, left_stats, right_stats, left_root, right_root)
    *of_blocks, vec_grads, vec_accum_new, vec_new, grad_norm, output, input_grad = update(
        raw, window, norm_tile, shift, blocks_in, vectors.T, vec_accum.T, output, input_grad
    )
    return (output, input_grad, *of_blocks, vec_grads.T, vec_accum_new.T, vec_new.T, grad_norm.reshape(()))


def solution(mesh):
    rows, blocks, vecs = P(BOTH, None), P(BOTH, None, None), P(None, BOTH)
    return jax.shard_map(
        body,
        mesh=mesh,
        in_specs=(rows, rows, rows, P(), blocks, blocks, blocks, blocks, blocks, vecs, vecs),
        out_specs=(rows, rows, blocks, blocks, blocks, blocks, blocks, vecs, vecs, vecs, P()),
        check_vma=False,
    )
```

time: 208 us -> 182 us (0.88)
  Pallas kernels: 194 us -> 173 us
  local copies, waits for them, and re-layouts: 8.17 us -> 4.47 us
    pallas_call x2 -> x1, Pallas kernels: 189 us -> 170 us  [forward_backward(): pl.pallas_call(whole_kernel, out_shape=[jax.ShapeDtypeStruct((TOKENS, D),...]
    unnamed x33 -> x24, local copies, waits for them, and re-layouts: 6.15 us -> 4.47 us
where the time goes in v2:
time: 182 us; the launch traced here: 181 us
  Pallas kernels  173 us (95%)
  local copies, waits for them, and re-layouts  4.47 us (2%)
  other arithmetic  2.92 us (2%)
    pallas_call x1, Pallas kernels, forward_backward(): pl.pallas_call(whole_kernel, out_shape=[jax.ShapeDtypeStruct((TOKENS, D),...  170 us
    unnamed x24, local copies, waits for them, and re-layouts  4.47 us

profile of v2, /device:TPU:1, one launch (start us, length us, event | category | flops | bytes accessed | tf_op | source)
XLA Modules:
  0.0 181.2 jit_solution(846275959249914718)
XLA Ops:
  0.7 1.6 select_reduce_fusion.block_at
  2.3 1.3 fusion.3
  3.6 0.0 copy-start.2
  3.6 0.0 copy-start.3
  3.6 0.0 copy-start.4
  3.6 0.0 copy-start.5
  3.6 0.0 copy-start.6
  3.6 0.0 copy-start.9
  3.6 0.0 copy-start.10
  3.6 170.0 %forward_backward.1 = (bf16[245,1024]{1,0:T(8,128)(2,1)}, bf16[245,1024]{1,0:T(8,128)(2,1)}, f32[6,128,128]{2,1,0:T(8,128)}, f32[2,8,128]{2,1,0:T(8,128)}, f32[8,128]{1,0:T(8,128)}) custom-call(s32[768]{0:T(1024)} %select_reduce_fusion.block_at, s32[768]{0:T(1024)} %get-tuple-element.44.left_at, s32[768]{0:T(1024)} %get-tuple-element.43.right_at, ...), custom_call_target="tpu_custom_call" | custom-call | flops 19000000512 | bytes 10000000 | tf_op jit(solution)/shard_map/forward_backward/pallas_call | solution.py:852
  173.6 0.0 copy-done.2
  173.6 0.0 copy-done.3
  173.6 0.0 copy-done.4
  173.7 0.0 copy-done.5
  173.7 0.0 copy-done.6
  173.7 0.0 copy-done.9
  173.7 0.0 copy-done.10
  173.7 0.0 copy-start
  173.7 1.0 copy-done
  174.7 1.0 copy-done.1
  175.8 1.0 copy-done.7
  176.8 0.7 copy-done.8
  177.5 0.7 copy-done.11
  178.1 2.9 %update.1 = (f32[6,128,128]{2,1,0:T(8,128)}, f32[6,128,128]{2,1,0:T(8,128)}, f32[6,128,128]{2,1,0:T(8,128)}, f32[6,128,128]{2,1,0:T(8,128)}, bf16[6,128,128]{2,1...) custom-call(f32[6,128,128]{2,1,0:T(8,128)S(1)} %copy-done.7, ...), custom_call_target="tpu_custom_call" | custom-call | tf_op jit(solution)/shard_map/update/pallas_call | solution.py:950
  (4 shorter events, 0.0 us)
Async XLA Ops:
  3.6 170.0 %copy-start.2 = (f32[6,128,128]{2,1,0:T(8,128)S(1)}, f32[6,128,128]{2,1,0:T(8,128)}, u32[]{:S(2)}) copy-start(f32[6,128,128]{2,1,0:T(8,128)} %master.1) | copy-start | bytes 1179652
  3.6 170.0 %copy-start.3 = (f32[6,128,128]{2,1,0:T(8,128)S(1)}, f32[6,128,128]{2,1,0:T(8,128)}, u32[]{:S(2)}) copy-start(f32[6,128,128]{2,1,0:T(8,128)} %left_stats.1) | copy-start | bytes 1179652
  3.6 170.1 %copy-start.4 = (f32[6,128,128]{2,1,0:T(8,128)S(1)}, f32[6,128,128]{2,1,0:T(8,128)}, u32[]{:S(2)}) copy-start(f32[6,128,128]{2,1,0:T(8,128)} %right_stats.1) | copy-start | bytes 1179652
  3.6 170.1 %copy-start.5 = (f32[6,128,128]{2,1,0:T(8,128)S(1)}, f32[6,128,128]{2,1,0:T(8,128)}, u32[]{:S(2)}) copy-start(f32[6,128,128]{2,1,0:T(8,128)} %left_root.1) | copy-start | bytes 1179652
  3.6 170.1 %copy-start.6 = (f32[6,128,128]{2,1,0:T(8,128)S(1)}, f32[6,128,128]{2,1,0:T(8,128)}, u32[]{:S(2)}) copy-start(f32[6,128,128]{2,1,0:T(8,128)} %right_root.1) | copy-start | bytes 1179652
  3.6 170.1 %copy-start.9 = (f32[12,8]{0,1:T(8,128)S(1)}, f32[12,8]{0,1:T(8,128)}, u32[]{:S(2)}) copy-start(f32[12,8]{0,1:T(8,128)} %param.21) | copy-start | bytes 1156
  3.6 170.1 %copy-start.10 = (f32[12,8]{0,1:T(8,128)S(1)}, f32[12,8]{0,1:T(8,128)}, u32[]{:S(2)}) copy-start(f32[12,8]{0,1:T(8,128)} %param.22) | copy-start | bytes 1156
  173.7 1.0 copy-start
  174.7 1.0 copy-start.1
  175.8 1.0 copy-start.7
  176.8 0.7 copy-start.8
  177.5 0.7 copy-start.11

commit v3 on v2

--- a/solution.py
+++ b/solution.py
@@ -95,8 +95,8 @@
     pl.semaphore_wait(semaphore, len(plane + column))
 
 
-def loop(count, body):
-    lax.fori_loop(0, count, lambda i, _: (body(i), None)[1], None)
+def loop(count, body, together=1):
+    lax.fori_loop(0, count, lambda i, _: (body(i), None)[1], None, unroll=together)
 
 
 def dot(left, right):
@@ -267,22 +267,25 @@
 
 
 def pass_kernel(
-    block_at, master_in, vectors_in, patches, keep_in, cotangent, output, input_grad, vec_out,
+    owner_in, places_in, master_in, vectors_in, patches, keep_in, cotangent, output, input_grad, master, vec_out,
     g, left, right, flats, q, k, v, att, a_low, probs, act, w_out, wall, sums, vec,
-    master, vectors, keep, send_sem, recv_sem, held_sem, ready,
+    vectors, keep, owner, places, made, tables, send_sem, recv_sem, held_sem, ready,
 ):
     tokens, d_mid, mid, d_a = (flats.at[i] for i in range(4))
     loads = [
         pltpu.make_async_copy(src, to, held_sem.at[i])
         for i, (src, to) in enumerate(
-            ((master_in, master), (vectors_in, vectors), (patches, output), (cotangent, input_grad), (keep_in, keep))
+            (
+                (master_in, master), (vectors_in, vectors), (patches, output), (cotangent, input_grad), (keep_in, keep),
+                (owner_in, owner), (places_in, places),
+            )
         )
     ]
     for load in loads:
         load.start()
 
     def block(n):
-        return g[pl.ds(block_at[n], 8)].reshape(SIDE, SIDE)
+        return g[pl.ds(tables[lax.div(n, 128), lax.rem(n, 128)], 8)].reshape(SIDE, SIDE)
 
     def columns(m, j, count):
         rows = (256 if m == 4 else 64 if m < 4 else 256) // WIDTH[m]
@@ -326,9 +329,37 @@
             right[64 + c, strip(i), :] = cot[:, c * 128 : (c + 1) * 128].astype(BF16)
         add_sums(7, cot)
 
+    def make_tables():
+        number = owner[...]
+        matrix = sum((number >= first).astype(jnp.int32) for first in FIRST[1:])
+
+        def by_matrix(values):
+            return sum(jnp.where(matrix == m, value, 0) for m, value in enumerate(values))
+
+        inner = number - by_matrix(FIRST)
+        wide_one = matrix == 4
+        made[8:14, :] = by_matrix(LEFT_AT) + jnp.where(wide_one, inner >> 5, inner >> 3)
+        made[16:22, :] = by_matrix(RIGHT_AT) + jnp.where(wide_one, inner & 31, inner & 7)
+        lane = lax.broadcasted_iota(jnp.int32, (128, 128), 1)
+        found = [jnp.zeros((8, 128), F32)] * 6
+        for i in range(6):
+            held_by = jnp.broadcast_to(number[i : i + 1].astype(F32), (128, 128)).T
+            lies_at = jnp.broadcast_to(places[i : i + 1, :].astype(F32), (128, 128)).T
+            for j in range(6):
+                hit = held_by == (lane + 128 * j).astype(F32)
+                found[j] = found[j] + by_eights(jnp.where(hit, lies_at, 0.0))
+        for j in range(6):
+            at = jnp.sum(found[j], 0, keepdims=True).astype(jnp.int32)
+            made[j : j + 1, :] = jnp.clip(at, 0, ALL_ROWS - 8)
+
     def meanwhile():
+        for load in loads[5:]:
+            load.wait()
+        make_tables()
+        to_scalars = pltpu.make_async_copy(made, tables, held_sem.at[7])
+        to_scalars.start()
         sums[...] = jnp.zeros_like(sums)
-        for load in loads[2:]:
+        for load in loads[2:5]:
             load.wait()
         for came, to in ((output, tokens), (input_grad, d_mid)):
             to[0:TOKENS, :] = came[...].astype(F32)
@@ -352,7 +383,8 @@
         wall[...] = jnp.where(
             image(row_at) == image(col_at), jnp.broadcast_to(dropped, (ROWS, ROWS)) * MASKED, OUTSIDE
         )
-        loop(8, first_normal)
+        loop(8, first_normal, 2)
+        to_scalars.wait()
 
     barrier = pltpu.get_barrier_semaphore()
     announce(barrier)
@@ -366,7 +398,7 @@
     def first_norm(i):
         a_low[strip(i), :] = (d_a[strip(i), :] * line(0) + line(1)).astype(BF16)
 
-    loop(8, first_norm)
+    loop(8, first_norm, 4)
 
     def project(j):
         left[pl.ds(2 * j, 2)] = a_low[:, lanes(j, 256)].T.reshape(2, 128, ROWS)
@@ -375,7 +407,7 @@
         k[:, at] = dot(a_low[...], columns(1, 2 * j, 2)).astype(BF16)
         v[:, at] = (dot(a_low[...], columns(2, 2 * j, 2)) + vec[3:4, at]).astype(BF16)
 
-    loop(4, project)
+    loop(4, project, 4)
 
     low_half = lax.broadcasted_iota(jnp.int32, (ROWS, 128), 1) < HEAD_DIM
 
@@ -399,19 +431,19 @@
         att[:, at] = pair
         left[8 + j] = pair.T
 
-    loop(8, attend)
+    loop(8, attend, 4)
 
     def to_mid(j):
         at = lanes(j, 256)
         mid[:, at] = tokens[:, at] + (dot(att[...], columns(3, 2 * j, 2)) + vec[4:5, at])
 
-    loop(4, to_mid)
+    loop(4, to_mid, 4)
 
     def second_norm(i):
         n, _ = normal(mid[strip(i), :])
         a_low[strip(i), :] = (n * line(5) + line(6)).astype(BF16)
 
-    loop(8, second_norm)
+    loop(8, second_norm, 8)
 
     def hidden(j):
         pre = dot(a_low[...], columns(4, 2 * j, 2)) + vec[pl.ds(8 + j // 4, 1), lanes(j % 4, 256)]
@@ -427,14 +459,14 @@
         right[33 + 2 * j] = d_pre[:, 128:]
         add_sums(8 + j // 4, d_pre.astype(F32), lanes(j % 4, 256))
 
-    loop(16, hidden)
+    loop(16, hidden, 4)
 
     def second_back(j):
         at = lanes(j, 256)
         left[pl.ds(16 + 2 * j, 2)] = a_low[:, at].T.reshape(2, 128, ROWS)
         d_a[:, at] = dot_nt(stack(32, 32), rows_of(4, 2 * j, 2))
 
-    loop(4, second_back)
+    loop(4, second_back, 4)
 
     def mid_back(i):
         rows = strip(i)
@@ -451,12 +483,12 @@
         add_sums(6, d)
         add_sums(4, low.astype(F32))
 
-    loop(8, mid_back)
+    loop(8, mid_back, 8)
 
     def att_back(j):
         att[:, lanes(j, 256)] = dot_nt(stack(24, 8), rows_of(3, 2 * j, 2)).astype(BF16)
 
-    loop(4, att_back)
+    loop(4, att_back, 4)
 
     def heads_back(j):
         at = lanes(j, 128)
@@ -479,13 +511,13 @@
         add_sums(2, d_q.astype(F32), at)
         add_sums(3, d_v.astype(F32), at)
 
-    loop(8, heads_back)
+    loop(8, heads_back, 4)
 
     def first_back(j):
         weights = jnp.concatenate([rows_of(m, 2 * j, 2) for m in range(3)], 1)
         d_a[:, lanes(j, 256)] = dot_nt(stack(0, 24), weights)
 
-    loop(4, first_back)
+    loop(4, first_back, 4)
 
     def token_back(i):
         rows = strip(i)
@@ -500,7 +532,7 @@
     for copy in sends:
         copy.wait_send()
     announce(ready)
-    loop(8, token_back)
+    loop(8, token_back, 8)
     input_grad[...] = d_mid[0:TOKENS, :].astype(BF16)
     folded = jnp.sum(sums[...], 1)
     vec_out[0] = folded[:8]
@@ -519,9 +551,15 @@
 )
 AHEAD = 1
 RING = 2 * AHEAD + 2
+OUT_RING = 6
+OUT_ROUNDS = tuple(round_ for round_ in ROUNDS if round_[0])
 
 
 VMEM_LIMIT = 62 * MIB
+
+
+def in_hbm(array):
+    return pltpu.with_memory_space_constraint(array, pltpu.HBM)
 
 
 class Rows:
@@ -542,9 +580,9 @@
 
 
 def scatter_kernel(
-    left_at, right_at, left, right, vec_in,
+    tables, left, right, vec_in,
     total, window, norm_tile,
-    g, kept, b_out, b_in, b_half, a_out, a_in,
+    g, kept, a_out, a_in,
     vec_y, vec_y_in, vec_x, vec_x_in, vec_z, vec_z_in, vec_t, tiles,
     tw_send, tw_recv, c_send, c_recv, b_send, b_recv, a_send, a_recv, v_send, v_recv, n_send, n_recv,
     between,
@@ -553,7 +591,15 @@
     twin = device(pos, 1 - core)
     axes = [[device(moved(pos, a, s), core) for s in (1, 2, 3)] for a in range(3)]
     plane, column = partners()
-    tw_out, tw_in, c_out, c_in, c_half = (Rows(g, at) for at in (0, 3 * RING, 6 * RING, 6 * RING + 36, 6 * RING + 60))
+    sizes, at = (3 * RING, 3 * RING, 3 * OUT_RING, 24, 12, 9, 6, 3), 0
+    places = []
+    for size in sizes:
+        places.append(Rows(g, at))
+        at += size
+    tw_out, tw_in, c_out, c_in, c_half, b_out, b_in, b_half = places
+
+    def out_row(p, round_):
+        return 3 * (OUT_ROUNDS.index(round_) % OUT_RING) + p
 
     def pick(options, i):
         value = options[-1]
@@ -578,7 +624,8 @@
         slot = (wide * 8 + narrow) * 6 + 2 * p
         made = []
         for i in range(2):
-            made.append(dot(left[left_at[slot + i]], right[right_at[slot + i]]))
+            row, lane = lax.div(slot + i, 128), lax.rem(slot + i, 128)
+            made.append(dot(left[tables[8 + row, lane]], right[tables[16 + row, lane]]))
         return jnp.concatenate(made, 0)
 
     def remote(src, dst, send_sem, recv_sem, to):
@@ -607,26 +654,38 @@
     def c_half_copy(p, bi, second):
         n = p * 4 + bi
         return remote(
-            c_out.half(n, second), c_half.half(n, second), c_send.at[2 * n + second], c_recv.at[2 * n + second],
+            c_out.half(out_row(p, (2, bi)), second), c_half.half(n, second), c_send.at[2 * n + second], c_recv.at[2 * n + second],
             neighbour(p, 2, 3 if second else 1),
         )
 
     def c_whole_copy(p, bi, leftward):
         n = 12 * leftward + p * 4 + bi
         return remote(
-            c_out.row(12 + n), c_in.row(n), c_send.at[24 + n], c_recv.at[24 + n], neighbour(p, 2, 3 if leftward else 1)
-        )
+            c_out.row(out_row(p, (1 + 2 * leftward, bi))), c_in.row(n), c_send.at[24 + n], c_recv.at[24 + n], neighbour(p, 2, 3 if leftward else 1)
+        )
+
+    def free_out(p, round_):
+        before = OUT_ROUNDS.index(round_) - OUT_RING
+        if before >= 0:
+            left_out(p, OUT_ROUNDS[before])
+
+    def left_out(p, round_):
+        ci, bi = round_
+        if ci == 2:
+            c_half_copy(p, bi, 0).wait_send()
+            c_half_copy(p, bi, 1).wait_send()
+        else:
+            c_whole_copy(p, bi, ci // 2).wait_send()
 
     def b_half_copy(p, second):
-        part = pl.ds(2 * second, 2)
         return remote(
-            b_out.at[p, 0, part], b_half.at[p, part], b_send.at[4 * p + second], b_recv.at[4 * p + second],
+            b_out.half(3 * p, second), b_half.half(p, second), b_send.at[4 * p + second], b_recv.at[4 * p + second],
             neighbour(p, 1, 3 if second else 1),
         )
 
     def b_whole_copy(p, leftward):
         return remote(
-            b_out.at[p, 1 + leftward], b_in.at[p, leftward], b_send.at[4 * p + 2 + leftward],
+            b_out.row(3 * p + 1 + leftward), b_in.row(2 * p + leftward), b_send.at[4 * p + 2 + leftward],
             b_recv.at[4 * p + 2 + leftward], neighbour(p, 1, 3 if leftward else 1),
         )
 
@@ -636,8 +695,9 @@
 
     def opposite_row(k, p):
         _, bi = ROUNDS[k]
+        free_out(p, ROUNDS[k])
         for ai in range(4):
-            c_out.put(p * 4 + bi, ai, chip_sum(k, p, ai))
+            c_out.put(out_row(p, ROUNDS[k]), ai, chip_sum(k, p, ai))
             if ai % 2:
                 c_half_copy(p, bi, ai // 2).start()
 
@@ -646,11 +706,12 @@
         leftward = ci // 2
         n = p * 4 + bi
         c_half_copy(p, bi, leftward).wait_recv()
+        free_out(p, ROUNDS[k])
         for ai in range(4):
             value = chip_sum(k, p, ai)
             if ai // 2 == leftward:
                 value = value + c_half.get(n, ai)
-            c_out.put(12 + 12 * leftward + n, ai, value)
+            c_out.put(out_row(p, ROUNDS[k]), ai, value)
         c_whole_copy(p, bi, leftward).start()
 
     def own_row(k, p):
@@ -667,8 +728,8 @@
                 kept[p, :, ai * 128 : (ai + 1) * 128] = value
                 continue
             if bi % 2 and ai // 2 == leftward:
-                value = value + b_half[p, ai].astype(F32)
-            b_out[p, 0 if bi == 2 else 1 + leftward, ai] = value.astype(BF16)
+                value = value + b_half.get(p, ai)
+            b_out.put(3 * p + (0 if bi == 2 else 1 + leftward), ai, value)
             if bi == 2 and ai % 2:
                 b_half_copy(p, ai // 2).start()
         if bi % 2:
@@ -733,7 +794,7 @@
         between(k)
 
     def row_sum(p, ai):
-        return kept[p, :, ai * 128 : (ai + 1) * 128] + b_in[p, 0, ai].astype(F32) + b_in[p, 1, ai].astype(F32)
+        return kept[p, :, ai * 128 : (ai + 1) * 128] + b_in.get(2 * p, ai) + b_in.get(2 * p + 1, ai)
 
     def last_axis(p):
         b_whole_copy(p, 0).wait_recv()
@@ -780,10 +841,9 @@
     def sent(p):
         for k in range(len(ROUNDS) - RING, len(ROUNDS)):
             twin_copy(k, p).wait_send()
+        for round_ in OUT_ROUNDS[-OUT_RING:]:
+            left_out(p, round_)
         for side in (0, 1):
-            for bi in range(4):
-                c_half_copy(p, bi, side).wait_send()
-                c_whole_copy(p, bi, side).wait_send()
             b_half_copy(p, side).wait_send()
             b_whole_copy(p, side).wait_send()
         for by in (1, 2, 3):
@@ -801,7 +861,7 @@
 
 
 def whole_kernel(
-    block_at, left_at, right_at, master_in, vectors_in, patches, keep_in, cotangent,
+    owner, places, master_in, vectors_in, patches, keep_in, cotangent,
     output, input_grad, total, window, norm_tile, *scratch,
 ):
     gathered, scattered = scratch[:PASS_SCRATCH], scratch[PASS_SCRATCH:]
@@ -809,7 +869,7 @@
     vec_in, *scattered = scattered
     ready = gathered[-1]
     last = pass_kernel(
-        block_at, master_in, vectors_in, patches, keep_in, cotangent, output, input_grad, vec_in, *gathered
+        owner, places, master_in, vectors_in, patches, keep_in, cotangent, output, input_grad, total, vec_in, *gathered
     )
     all_announced(ready)
 
@@ -817,16 +877,16 @@
         if 1 <= k <= 4:
             last(k - 1)
 
-    scatter_kernel(left_at, right_at, left, right, vec_in, total, window, norm_tile, g, flats, *scattered, between)
+    scatter_kernel(gathered[TABLES], left, right, vec_in, total, window, norm_tile, g, flats, *scattered, between)
     output[...] = flats[3, 0:TOKENS, :].astype(BF16)
 
 
-PASS_SCRATCH = 22
-
-
-def forward_backward(block_at, left_at, right_at, master, vectors, patches, keep, cotangent):
+PASS_SCRATCH, TABLES = 25, 20
+
+
+def forward_backward(*operands):
     vmem = pl.BlockSpec(memory_space=pltpu.VMEM)
-    flat, row = (ROWS, D), (4, 256, 128)
+    flat = (ROWS, D)
     dma = pltpu.SemaphoreType.DMA
     pass_scratch = [
         pltpu.VMEM((ALL_ROWS, 16, 128), BF16),
@@ -840,12 +900,15 @@
         pltpu.VMEM((ROWS, ROWS), F32),
         pltpu.VMEM((NV, 8, D), F32),
         pltpu.VMEM((16, D), F32),
-        pltpu.VMEM((6, SIDE, SIDE), F32),
         pltpu.VMEM((8, NV), F32),
         pltpu.VMEM((IMAGES, PATCHES), jnp.int32),
+        pltpu.VMEM((6, 128), jnp.int32),
+        pltpu.VMEM((6, 128), jnp.int32),
+        pltpu.VMEM((24, 128), jnp.int32),
+        pltpu.SMEM((24, 128), jnp.int32),
         dma((3, 40)),
         dma((3, 40)),
-        dma((5,)),
+        dma((8,)),
         pltpu.SemaphoreType.REGULAR,
     ]
     assert len(pass_scratch) == PASS_SCRATCH
@@ -858,14 +921,11 @@
             jax.ShapeDtypeStruct((2, 8, 128), F32),
             jax.ShapeDtypeStruct((8, 128), F32),
         ],
-        in_specs=[pl.BlockSpec(memory_space=pltpu.SMEM)] * 3 + [pl.BlockSpec(memory_space=pltpu.HBM)] * 5,
+        in_specs=[pl.BlockSpec(memory_space=pltpu.HBM)] * 7,
         out_specs=[vmem] * 5,
         scratch_shapes=pass_scratch
         + [
             pltpu.VMEM((2, 8, D), F32),
-            pltpu.VMEM((3, 3, *row), BF16),
-            pltpu.VMEM((3, 2, *row), BF16),
-            pltpu.VMEM((3, *row), BF16),
             pltpu.VMEM((9, 256, 128), BF16),
             pltpu.VMEM((9, 256, 128), BF16),
             pltpu.VMEM((4, 8, 256), F32),
@@ -886,7 +946,7 @@
             flops=19_000_000_000, bytes_accessed=10_000_000, transcendentals=3_000_000
         ),
         name="forward_backward",
-    )(block_at, left_at, right_at, master, vectors, patches, keep, cotangent)
+    )(*(in_hbm(operand) for operand in operands))
 
 
 def rounded_dot(left, right, over):
@@ -899,18 +959,23 @@
     raw, window, norm_tile, shift, master, left_stats, right_stats, left_root, right_root, vectors, vec_accum,
     output_in, input_grad_in,
     block_grads, new_left, new_right, new_master, new_copy, vec_grads, vec_accum_new, vec_new, grad_norm,
-    output, input_grad, sem,
+    output, input_grad, passing, sem,
 ):
-    def copies():
-        pairs = ((output_in, output), (input_grad_in, input_grad))
-        return [pltpu.make_async_copy(src, dst, sem.at[i]) for i, (src, dst) in enumerate(pairs)]
+    def copies(way):
+        ends = ((output_in, output), (input_grad_in, input_grad))
+        return [
+            pltpu.make_async_copy(
+                passing.at[i] if way else pair[0], pair[1] if way else passing.at[i], sem.at[2 * way + i]
+            )
+            for i, pair in enumerate(ends)
+        ]
 
     norm = jnp.sqrt(jnp.sum(norm_tile[...], keepdims=True))
     clip = 1.0 / jnp.maximum(norm, 1.0)
 
     @pl.when(pl.program_id(0) == 0)
     def _():
-        for copy in copies():
+        for copy in copies(0):
             copy.start()
         grad_norm[...] = norm
         lanes = pltpu.roll(window[...].reshape(16, 128), shift[0], 1)
@@ -930,16 +995,22 @@
         new_master[i] = master_now
         new_copy[i] = master_now.astype(BF16)
 
+    @pl.when(pl.program_id(0) == 0)
+    def _():
+        for came, copy in zip(copies(0), copies(1)):
+            came.wait()
+            copy.start()
+
     @pl.when(pl.program_id(0) == pl.num_programs(0) - 1)
     def _():
-        for copy in copies():
+        for copy in copies(1):
             copy.wait()
 
 
 def update(raw, window, norm_tile, shift, blocks_in, vectors, vec_accum, output, input_grad):
     per = 2
     blocks = pl.BlockSpec((per, SIDE, SIDE), lambda i: (i, 0, 0))
-    anywhere = pl.BlockSpec(memory_space=pl.ANY)
+    anywhere = pl.BlockSpec(memory_space=pltpu.HBM)
 
     def whole(*shape):
         return pl.BlockSpec(shape, lambda i: (0,) * len(shape))
@@ -960,32 +1031,18 @@
         + [whole(8, NV)] * 2
         + [anywhere] * 2,
         out_specs=[blocks] * 5 + [whole(8, NV)] * 3 + [whole(1, 1)] + [anywhere] * 2,
-        scratch_shapes=[pltpu.SemaphoreType.DMA((2,))],
+        scratch_shapes=[pltpu.VMEM((2, TOKENS, D), BF16), pltpu.SemaphoreType.DMA((4,))],
         compiler_params=pltpu.CompilerParams(vmem_limit_bytes=32 * MIB),
         name="update",
-    )(raw, window, norm_tile, shift, *blocks_in, vectors, vec_accum, output, input_grad)
+    )(*(in_hbm(a) for a in (raw, window, norm_tile)), shift, *blocks_in, vectors, vec_accum, in_hbm(output), in_hbm(input_grad))
 
 
 def body(
     patches, keep, cotangent, owner_table, master, left_stats, right_stats, left_root, right_root, vectors, vec_accum,
 ):
     wide, narrow = lax.axis_index("wide"), lax.axis_index("narrow")
-    numbers = jnp.arange(NBLK, dtype=jnp.int32)
-    held = owner_table[None, :] == numbers[:, None]
-    block_at = jnp.sum(jnp.where(held, jnp.asarray(BLOCK_AT)[None, :], 0), 1)
-    matrix = sum((owner_table >= first).astype(jnp.int32) for first in FIRST[1:])
-
-    def by_matrix(values):
-        return sum(jnp.where(matrix == m, value, 0) for m, value in enumerate(values))
-
-    inner = owner_table - by_matrix(FIRST)
-    block_row = jnp.where(matrix == 4, inner // 32, inner // 8)
-    block_column = jnp.where(matrix == 4, inner % 32, inner % 8)
-    left_at = by_matrix(LEFT_AT) + block_row
-    right_at = by_matrix(RIGHT_AT) + block_column
-
     output, input_grad, raw, window, norm_tile = forward_backward(
-        block_at, left_at, right_at, master, vectors.T, patches, keep, cotangent
+        owner_table.reshape(6, 128), jnp.asarray(BLOCK_AT.reshape(6, 128)), master, vectors.T, patches, keep, cotangent
     )
     lane = ((wide % 2) * 8 + narrow) * 8
     shift = jnp.reshape((128 - lane) % 128, (1,)).astype(jnp.int32)

time: 182 us -> 165 us (0.907)
  Pallas kernels: 173 us -> 163 us
  local copies, waits for them, and re-layouts: 4.47 us -> 0.66 us
  other arithmetic: 2.92 us -> 0 us
    pallas_call x1, Pallas kernels: 170 us -> 159 us  [forward_backward(): pl.pallas_call(whole_kernel, out_shape=[jax.ShapeDtypeStruct((TOKENS, D),...]
    unnamed x24 -> x14, local copies, waits for them, and re-layouts: 4.47 us -> 0.66 us
where the time goes in v3:
time: 165 us
  Pallas kernels  163 us (99%)
    pallas_call x1, Pallas kernels, forward_backward(): pl.pallas_call(whole_kernel, out_shape=[jax.ShapeDtypeStruct((TOKENS, D),...  159 us
    pallas_call x1, Pallas kernels, update(): pl.pallas_call(step_kernel, grid=(6 // per,), out_shape=[f32_blocks] * 4...  4.65 us

profile of v3, /device:TPU:1, one launch (start us, length us, event | category | flops | bytes accessed | tf_op | source)
XLA Modules:
  0.0 165.0 jit_solution(17027719098376608987)
XLA Ops:
  0.7 0.0 copy-start
  0.7 0.0 copy-start.1
  0.7 0.0 copy-start.2
  0.7 0.0 copy-start.3
  0.7 0.0 copy-start.4
  0.7 158.7 %forward_backward.1 = (bf16[245,1024]{1,0:T(8,128)(2,1)}, bf16[245,1024]{1,0:T(8,128)(2,1)}, f32[6,128,128]{2,1,0:T(8,128)}, f32[2,8,128]{2,1,0:T(8,128)}, f32[8,128]{1,0:T(8,128)}) custom-call(s32[6,128]{1,0:T(8,128)} %bitcast.11, s32[6,128]{1,0:T(8,128)} %constant.36.clone.places, f32[6,128,128]{2,1,0:T(8,128)} %master.1, f32[8,12]{1,0:T(8,128)} %bitcast.8, ...), custom_call_target="tpu_custom_call" | custom-call | flops 19000000512 | bytes 10000000 | tf_op jit(solution)/shard_map/forward_backward/pallas_call | solution.py:915
  159.4 0.0 copy-start.6
  159.5 0.0 copy-start.5
  159.5 0.0 copy-done
  159.5 0.0 copy-done.1
  159.5 0.0 copy-done.2
  159.5 0.0 copy-done.3
  159.5 0.0 copy-done.4
  159.5 0.6 copy-done.6
  160.1 0.0 copy-done.5
  160.2 4.7 %update.1 = (f32[6,128,128]{2,1,0:T(8,128)}, f32[6,128,128]{2,1,0:T(8,128)}, f32[6,128,128]{2,1,0:T(8,128)}, f32[6,128,128]{2,1,0:T(8,128)}, bf16[6,128,128]{2,1...) custom-call(f32[6,128,128]{2,1,0:T(8,128)} %get-tuple-element.27.raw, ...), custom_call_target="tpu_custom_call" | custom-call | tf_op jit(solution)/shard_map/update/pallas_call | solution.py:1021
Async XLA Ops:
  0.7 158.8 %copy-start = (f32[6,128,128]{2,1,0:T(8,128)S(1)}, f32[6,128,128]{2,1,0:T(8,128)}, u32[]{:S(2)}) copy-start(f32[6,128,128]{2,1,0:T(8,128)} %master.1) | copy-start | bytes 1179652
  0.7 158.8 %copy-start.1 = (f32[6,128,128]{2,1,0:T(8,128)S(1)}, f32[6,128,128]{2,1,0:T(8,128)}, u32[]{:S(2)}) copy-start(f32[6,128,128]{2,1,0:T(8,128)} %left_stats.1) | copy-start | bytes 1179652
  0.7 158.8 %copy-start.2 = (f32[6,128,128]{2,1,0:T(8,128)S(1)}, f32[6,128,128]{2,1,0:T(8,128)}, u32[]{:S(2)}) copy-start(f32[6,128,128]{2,1,0:T(8,128)} %right_stats.1) | copy-start | bytes 1179652
  0.7 158.8 %copy-start.3 = (f32[6,128,128]{2,1,0:T(8,128)S(1)}, f32[6,128,128]{2,1,0:T(8,128)}, u32[]{:S(2)}) copy-start(f32[6,128,128]{2,1,0:T(8,128)} %left_root.1) | copy-start | bytes 1179652
  0.7 158.8 %copy-start.4 = (f32[6,128,128]{2,1,0:T(8,128)S(1)}, f32[6,128,128]{2,1,0:T(8,128)}, u32[]{:S(2)}) copy-start(f32[6,128,128]{2,1,0:T(8,128)} %right_root.1) | copy-start | bytes 1179652
  159.4 0.7 copy-start.6
  159.5 0.7 copy-start.5

commit v4 on v3

--- a/solution.py
+++ b/solution.py
@@ -84,15 +84,18 @@
     return plane, column
 
 
-def announce(semaphore):
-    plane, column = partners()
-    for partner in plane + column:
-        pl.semaphore_signal(semaphore, inc=1, device_id=partner, device_id_type=MESH)
-
-
-def all_announced(semaphore):
-    plane, column = partners()
-    pl.semaphore_wait(semaphore, len(plane + column))
+def neighbours():
+    pos, core = place()
+    return [device(pos, 1 - core)] + [device(moved(pos, a, s), core) for a in range(3) for s in (1, -1)]
+
+
+def announce(semaphore, others):
+    for other in others:
+        pl.semaphore_signal(semaphore, inc=1, device_id=other, device_id_type=MESH)
+
+
+def all_announced(semaphore, others):
+    pl.semaphore_wait(semaphore, len(others))
 
 
 def loop(count, body, together=1):
@@ -239,19 +242,28 @@
         sides(p, 2)
     for p in parts:
         opposite(p, 0)
+    early = len(sends)
     for p in parts:
         sides(p, 3)
+
+    def from_twin(p, which):
+        _, b, c = spot(p)
+        for ci in range(4):
+            for bi in range(4):
+                if (ci == 2 or bi == 2) == which:
+                    arrived(at(p, 1 - core, c + ci, b + bi), p, 24 + 4 * ci + bi)
+
     for p in parts:
         opposite(p, 1)
         opposite(p, 2)
+        from_twin(p, False)
+    for copy in sends[:early]:
+        copy.wait_send()
     for p in parts:
         opposite(p, 3)
     for p in parts:
-        _, b, c = spot(p)
-        for ci in range(4):
-            for bi in range(4):
-                arrived(at(p, 1 - core, c + ci, b + bi), p, 24 + 4 * ci + bi)
-    return sends
+        from_twin(p, True)
+    return sends[early:]
 
 
 def normal(values):
@@ -268,10 +280,10 @@
 
 def pass_kernel(
     owner_in, places_in, master_in, vectors_in, patches, keep_in, cotangent, output, input_grad, master, vec_out,
-    g, left, right, flats, q, k, v, att, a_low, probs, act, w_out, wall, sums, vec,
+    g, left, right, flats, q, k, v, att, a_low, probs, w_qkv, w_out, wall, sums, vec,
     vectors, keep, owner, places, made, tables, send_sem, recv_sem, held_sem, ready,
 ):
-    tokens, d_mid, mid, d_a = (flats.at[i] for i in range(4))
+    tokens, d_mid, d_a, mid = (flats.at[i] for i in range(4))
     loads = [
         pltpu.make_async_copy(src, to, held_sem.at[i])
         for i, (src, to) in enumerate(
@@ -387,8 +399,8 @@
         to_scalars.wait()
 
     barrier = pltpu.get_barrier_semaphore()
-    announce(barrier)
-    all_announced(barrier)
+    announce(barrier, neighbours())
+    all_announced(barrier, neighbours())
     sends = gather_weights(master, vectors, loads[:2], g, send_sem, recv_sem, meanwhile)
 
     for w in range(8):
@@ -403,9 +415,14 @@
     def project(j):
         left[pl.ds(2 * j, 2)] = a_low[:, lanes(j, 256)].T.reshape(2, 128, ROWS)
         at = lanes(j, 256)
-        q[:, at] = (dot(a_low[...], columns(0, 2 * j, 2)) + vec[2:3, at]).astype(BF16)
-        k[:, at] = dot(a_low[...], columns(1, 2 * j, 2)).astype(BF16)
-        v[:, at] = (dot(a_low[...], columns(2, 2 * j, 2)) + vec[3:4, at]).astype(BF16)
+        made = []
+        for m in range(3):
+            weights = columns(m, 2 * j, 2)
+            w_qkv[m, :, at] = weights
+            made.append(dot(a_low[...], weights))
+        q[:, at] = (made[0] + vec[2:3, at]).astype(BF16)
+        k[:, at] = made[1].astype(BF16)
+        v[:, at] = (made[2] + vec[3:4, at]).astype(BF16)
 
     loop(4, project, 4)
 
@@ -450,7 +467,6 @@
         half = 0.5 * (1.0 + lax.erf(pre * math.sqrt(0.5)))
         slope = half + pre * (jnp.exp(-0.5 * pre * pre) * (1.0 / math.sqrt(2.0 * math.pi)))
         low = (pre * half).astype(BF16)
-        act[:, lanes(j, 256)] = low
         left[pl.ds(24 + 2 * j, 2)] = low.T.reshape(2, 128, ROWS)
         weights = rows_of(5, 2 * j, 2)
         w_out[lanes(j, 256), :] = weights
@@ -511,13 +527,14 @@
         add_sums(2, d_q.astype(F32), at)
         add_sums(3, d_v.astype(F32), at)
 
-    loop(8, heads_back, 4)
+    for copy in sends:
+        copy.wait_send()
+    announce(ready, sum(partners(), []))
 
     def first_back(j):
-        weights = jnp.concatenate([rows_of(m, 2 * j, 2) for m in range(3)], 1)
-        d_a[:, lanes(j, 256)] = dot_nt(stack(0, 24), weights)
-
-    loop(4, first_back, 4)
+        at = lanes(j, 256)
+        weights = jnp.concatenate([w_qkv[m, at, :] for m in range(3)], 1)
+        d_a[:, at] = dot_nt(stack(0, 24), weights)
 
     def token_back(i):
         rows = strip(i)
@@ -529,21 +546,24 @@
         add_sums(0, d * n)
         add_sums(1, d)
 
-    for copy in sends:
-        copy.wait_send()
-    announce(ready)
-    loop(8, token_back, 8)
-    input_grad[...] = d_mid[0:TOKENS, :].astype(BF16)
-    folded = jnp.sum(sums[...], 1)
-    vec_out[0] = folded[:8]
-    vec_out[1, 0 : NV - 8] = folded[8:]
-    vec_out[1, NV - 8 :] = jnp.zeros((16 - NV, D), F32)
-
-    def last(j):
-        at = lanes(j, 256)
-        d_a[:, at] = mid[:, at] + (dot(act[...], w_out[:, at]) + vec[7:8, at])
-
-    return last
+    def input_side(stage):
+        if stage < 2:
+            loop(2, lambda i: first_back(2 * stage + i), 2)
+        else:
+            loop(8, token_back, 8)
+            input_grad[...] = d_mid[0:TOKENS, :].astype(BF16)
+            folded = jnp.sum(sums[...], 1)
+            vec_out[0] = folded[:8]
+            vec_out[1, 0 : NV - 8] = folded[8:]
+            vec_out[1, NV - 8 :] = jnp.zeros((16 - NV, D), F32)
+
+    def output_side(stage):
+        fan = left[24 + 8 * stage : 32 + 8 * stage].reshape(D, ROWS)
+        mid[...] += dot_tn(fan, w_out[stage * D : (stage + 1) * D, :])
+        if stage == 3:
+            output[...] = (mid[...] + vec[7:8, :])[:TOKENS].astype(BF16)
+
+    return heads_back, input_side, output_side
 
 
 ROUNDS = (
@@ -585,7 +605,7 @@
     g, kept, a_out, a_in,
     vec_y, vec_y_in, vec_x, vec_x_in, vec_z, vec_z_in, vec_t, tiles,
     tw_send, tw_recv, c_send, c_recv, b_send, b_recv, a_send, a_recv, v_send, v_recv, n_send, n_recv,
-    between,
+    heads_back, between,
 ):
     pos, core = place()
     twin = device(pos, 1 - core)
@@ -614,19 +634,23 @@
         axis = axis_of(p, which)
         return tuple(pick([axes[a][by - 1][n] for a in range(3)], axis) for n in range(2))
 
-    def along(p, which, by):
-        return lax.rem(pick(pos, axis_of(p, which)) + by, 4)
-
-    def pair(p, ci, bi, ai, of_core):
-        spots = [along(p, 0, ai), along(p, 1, bi), along(p, 2, ci)]
-        x, y, z = (pick([spots[(a - s) % 3] for s in range(3)], p) for a in range(3))
-        wide, narrow = device((x, y, z), of_core)
-        slot = (wide * 8 + narrow) * 6 + 2 * p
-        made = []
-        for i in range(2):
-            row, lane = lax.div(slot + i, 128), lax.rem(slot + i, 128)
-            made.append(dot(left[tables[8 + row, lane]], right[tables[16 + row, lane]]))
-        return jnp.concatenate(made, 0)
+    adds = (lambda x: 16 * lax.div(x, 2) + 4 * lax.rem(x, 2), lambda y: 32 * y, lambda z: z)
+    share = [
+        [[adds[axis](lax.rem(pos[axis] + by, 4)) for by in range(4)] for axis in ORDERS[p]] for p in range(3)
+    ]
+
+    def row_pairs(k, p, of_core):
+        ci, bi = ROUNDS[k]
+        base = pick([share[i][2][ci] + share[i][1][bi] for i in range(3)], p) + 8 * of_core
+        pairs = []
+        for ai in range(4):
+            slot = (base + pick([share[i][0][ai] for i in range(3)], p)) * 6 + 2 * p
+            made = []
+            for i in range(2):
+                row, lane = lax.div(slot + i, 128), lax.rem(slot + i, 128)
+                made.append(dot(left[tables[8 + row, lane]], right[tables[16 + row, lane]]))
+            pairs.append(jnp.concatenate(made, 0))
+        return pairs
 
     def remote(src, dst, send_sem, recv_sem, to):
         return pltpu.make_async_remote_copy(
@@ -637,19 +661,17 @@
         n = 3 * (k % RING) + p
         return remote(tw_out.row(n), tw_in.row(n), tw_send.at[3 * k + p], tw_recv.at[3 * k + p], twin)
 
-    def for_twin(k, p):
+    def for_twin(k, p, pairs=None):
         if k >= len(ROUNDS):
             return
         if k >= RING:
             twin_copy(k - RING, p).wait_send()
-        ci, bi = ROUNDS[k]
-        for ai in range(4):
-            tw_out.put(3 * (k % RING) + p, ai, pair(p, ci, bi, ai, 1 - core))
+        for ai, value in enumerate(pairs or row_pairs(k, p, 1 - core)):
+            tw_out.put(3 * (k % RING) + p, ai, value)
         twin_copy(k, p).start()
 
-    def chip_sum(k, p, ai):
-        ci, bi = ROUNDS[k]
-        return pair(p, ci, bi, ai, core) + tw_in.get(3 * (k % RING) + p, ai)
+    def chip_sum(k, p, ai, pairs):
+        return pairs[ai] + tw_in.get(3 * (k % RING) + p, ai)
 
     def c_half_copy(p, bi, second):
         n = p * 4 + bi
@@ -693,28 +715,28 @@
         n = 3 * p + by - 1
         return remote(a_out.at[n], a_in.at[n], a_send.at[n], a_recv.at[n], neighbour(p, 0, by))
 
-    def opposite_row(k, p):
+    def opposite_row(k, p, pairs):
         _, bi = ROUNDS[k]
         free_out(p, ROUNDS[k])
         for ai in range(4):
-            c_out.put(out_row(p, ROUNDS[k]), ai, chip_sum(k, p, ai))
+            c_out.put(out_row(p, ROUNDS[k]), ai, chip_sum(k, p, ai, pairs))
             if ai % 2:
                 c_half_copy(p, bi, ai // 2).start()
 
-    def side_row(k, p):
+    def side_row(k, p, pairs):
         ci, bi = ROUNDS[k]
         leftward = ci // 2
         n = p * 4 + bi
         c_half_copy(p, bi, leftward).wait_recv()
         free_out(p, ROUNDS[k])
         for ai in range(4):
-            value = chip_sum(k, p, ai)
+            value = chip_sum(k, p, ai, pairs)
             if ai // 2 == leftward:
                 value = value + c_half.get(n, ai)
             c_out.put(out_row(p, ROUNDS[k]), ai, value)
         c_whole_copy(p, bi, leftward).start()
 
-    def own_row(k, p):
+    def own_row(k, p, pairs):
         _, bi = ROUNDS[k]
         n = p * 4 + bi
         leftward = bi // 2
@@ -723,7 +745,7 @@
         if bi % 2:
             b_half_copy(p, leftward).wait_recv()
         for ai in range(4):
-            value = chip_sum(k, p, ai) + c_in.get(n, ai) + c_in.get(12 + n, ai)
+            value = chip_sum(k, p, ai, pairs) + c_in.get(n, ai) + c_in.get(12 + n, ai)
             if bi == 0:
                 kept[p, :, ai * 128 : (ai + 1) * 128] = value
                 continue
@@ -760,7 +782,9 @@
         return remote(window.at[core], window.at[core], v_send.at[10], v_recv.at[10], twin)
 
     def vec_stage(stage):
-        if stage == 0:
+        if stage < 0:
+            vec_twin().start()
+        elif stage == 0:
             vec_twin().wait_recv()
             whole = vec_in[core] + vec_t[0]
             for i in range(4):
@@ -778,20 +802,42 @@
             window[core] = vec_sum(2, vec_z[...])
             vec_last().start()
 
-    vec_twin().start()
-    for k in range(AHEAD):
-        loop(3, lambda p: for_twin(k, p))
-    for k, (ci, _) in enumerate(ROUNDS):
+    def one_row(k, p, pairs=None):
+        pairs = pairs or row_pairs(k, p, core)
+        twin_copy(k, p).wait_recv()
+        ci = ROUNDS[k][0]
+        (own_row if ci == 0 else opposite_row if ci == 2 else side_row)(k, p, pairs)
+
+    x_low = lax.rem(pos[0], 2)
+
+    def class_at(i):
+        mine = jnp.where((i == 0) | ((i >= 2) & (i < 5)), x_low, 1 - x_low)
+        step = pick([2, 2, 0, 1, 3, 1, 0, 3], i)
+        return mine * 4 + lax.rem(pos[2] + step, 4)
+
+    def classes_back(first, count):
+        loop(count, lambda i: heads_back(class_at(first + i)), count)
+
+    classes_back(0, 2)
+    between(-1, vec_stage)
+    loop(2, lambda p: for_twin(0, p))
+    classes_back(2, 3)
+    for_twin(0, jnp.int32(2))
+    loop(2, lambda p: one_row(0, p))
+    classes_back(5, 3)
+    loop(2, lambda p: for_twin(1, p))
+    one_row(0, jnp.int32(2))
+    for_twin(1, jnp.int32(2))
+    for k in range(1, len(ROUNDS)):
 
         def one_round(p):
-            for_twin(k + AHEAD, p)
-            twin_copy(k, p).wait_recv()
-            (own_row if ci == 0 else opposite_row if ci == 2 else side_row)(k, p)
-
+            ahead = row_pairs(k + AHEAD, p, 1 - core) if k + AHEAD < len(ROUNDS) else None
+            pairs = row_pairs(k, p, core)
+            for_twin(k + AHEAD, p, ahead)
+            one_row(k, p, pairs)
+
+        between(k, vec_stage)
         loop(3, one_round)
-        if k % 3 == 2:
-            vec_stage(k // 3)
-        between(k)
 
     def row_sum(p, ai):
         return kept[p, :, ai * 128 : (ai + 1) * 128] + b_in.get(2 * p, ai) + b_in.get(2 * p + 1, ai)
@@ -827,16 +873,6 @@
         n = 15 * stage + i
         to = (column if stage else plane)[i]
         return remote(tiles.at[stage], tiles.at[2 + n], n_send.at[n], n_recv.at[n], to)
-
-    whole = squares
-    for stage, count in ((0, 15), (1, 7)):
-        tiles[stage] = whole
-        for i in range(count):
-            norm_copy(stage, i).start()
-        for i in range(count):
-            norm_copy(stage, i).wait_recv()
-            whole = whole + tiles[2 + 15 * stage + i]
-    norm_tile[...] = whole
 
     def sent(p):
         for k in range(len(ROUNDS) - RING, len(ROUNDS)):
@@ -849,12 +885,25 @@
         for by in (1, 2, 3):
             a_copy(p, by).wait_send()
 
-    loop(3, sent)
-    vec_twin().wait_send()
-    vec_last().wait_send()
-    for axis in range(3):
-        for by in (1, 2, 3):
-            vec_copy(axis, by).wait_send()
+    def all_sent():
+        loop(3, sent)
+        vec_twin().wait_send()
+        vec_last().wait_send()
+        for axis in range(3):
+            for by in (1, 2, 3):
+                vec_copy(axis, by).wait_send()
+
+    whole = squares
+    for stage, count in ((0, 15), (1, 7)):
+        tiles[stage] = whole
+        for i in range(count):
+            norm_copy(stage, i).start()
+        if stage == 0:
+            all_sent()
+        for i in range(count):
+            norm_copy(stage, i).wait_recv()
+            whole = whole + tiles[2 + 15 * stage + i]
+    norm_tile[...] = whole
     for stage, count in ((0, 15), (1, 7)):
         for i in range(count):
             norm_copy(stage, i).wait_send()
@@ -868,17 +917,25 @@
     g, left, right, flats = gathered[:4]
     vec_in, *scattered = scattered
     ready = gathered[-1]
-    last = pass_kernel(
+    heads_back, input_side, output_side = pass_kernel(
         owner, places, master_in, vectors_in, patches, keep_in, cotangent, output, input_grad, total, vec_in, *gathered
     )
-    all_announced(ready)
-
-    def between(k):
-        if 1 <= k <= 4:
-            last(k - 1)
-
-    scatter_kernel(gathered[TABLES], left, right, vec_in, total, window, norm_tile, g, flats, *scattered, between)
-    output[...] = flats[3, 0:TOKENS, :].astype(BF16)
+
+    def between(k, vec_stage):
+        if k < 0:
+            all_announced(ready, sum(partners(), []))
+        elif 1 <= k <= 3:
+            input_side(k - 1)
+            if k == 3:
+                vec_stage(-1)
+        elif 4 <= k <= 7:
+            output_side(k - 4)
+        if k in (5, 7, 9, 11):
+            vec_stage((k - 5) // 2)
+
+    scatter_kernel(
+        gathered[TABLES], left, right, vec_in, total, window, norm_tile, g, flats, *scattered, heads_back, between
+    )
 
 
 PASS_SCRATCH, TABLES = 25, 20
@@ -895,7 +952,7 @@
         pltpu.VMEM((4, *flat), F32),
         *[pltpu.VMEM(flat, BF16)] * 5,
         pltpu.VMEM((HEADS, ROWS, ROWS), BF16),
-        pltpu.VMEM((ROWS, FF), BF16),
+        pltpu.VMEM((3, D, D), BF16),
         pltpu.VMEM((FF, D), BF16),
         pltpu.VMEM((ROWS, ROWS), F32),
         pltpu.VMEM((NV, 8, D), F32),
@@ -1008,7 +1065,7 @@
 
 
 def update(raw, window, norm_tile, shift, blocks_in, vectors, vec_accum, output, input_grad):
-    per = 2
+    per = 3
     blocks = pl.BlockSpec((per, SIDE, SIDE), lambda i: (i, 0, 0))
     anywhere = pl.BlockSpec(memory_space=pltpu.HBM)
 
@@ -1034,7 +1091,7 @@
         scratch_shapes=[pltpu.VMEM((2, TOKENS, D), BF16), pltpu.SemaphoreType.DMA((4,))],
         compiler_params=pltpu.CompilerParams(vmem_limit_bytes=32 * MIB),
         name="update",
-    )(*(in_hbm(a) for a in (raw, window, norm_tile)), shift, *blocks_in, vectors, vec_accum, in_hbm(output), in_hbm(input_grad))
+    )(*(in_hbm(a) for a in (raw, window, norm_tile)), shift, *blocks_in, in_hbm(vectors), in_hbm(vec_accum), in_hbm(output), in_hbm(input_grad))
 
 
 def body(

time: 165 us -> 160 us (0.970)
  Pallas kernels: 163 us -> 158 us
    pallas_call x1, Pallas kernels: 159 us -> 155 us  [forward_backward(): pl.pallas_call(whole_kernel, out_shape=[jax.ShapeDtypeStruct((TOKENS, D),...]
where the time goes in v4:
time: 160 us; the launch traced here: 159 us
  Pallas kernels  158 us (99%)
    pallas_call x1, Pallas kernels, forward_backward(): pl.pallas_call(whole_kernel, out_shape=[jax.ShapeDtypeStruct((TOKENS, D),...  155 us
    pallas_call x1, Pallas kernels, update(): pl.pallas_call(step_kernel, grid=(6 // per,), out_shape=[f32_blocks] * 4...  3.94 us

profile of v4, /device:TPU:1, one launch (start us, length us, event | category | flops | bytes accessed | tf_op | source)
XLA Modules:
  0.0 159.4 jit_solution(11267880290065302714)
XLA Ops:
  0.7 0.0 copy-start
  0.7 0.0 copy-start.1
  0.7 0.0 copy-start.2
  0.7 0.0 copy-start.3
  0.7 0.0 copy-start.4
  0.7 154.5 %forward_backward.1 = (bf16[245,1024]{1,0:T(8,128)(2,1)}, bf16[245,1024]{1,0:T(8,128)(2,1)}, f32[6,128,128]{2,1,0:T(8,128)}, f32[2,8,128]{2,1,0:T(8,128)}, f32[8,128]{1,0:T(8,128)}) custom-call(s32[6,128]{1,0:T(8,128)} %bitcast.11, s32[6,128]{1,0:T(8,128)} %constant.36.clone.places, f32[6,128,128]{2,1,0:T(8,128)} %master.1, f32[8,12]{1,0:T(8,128)} %bitcast.8, ...), custom_call_target="tpu_custom_call" | custom-call | flops 19000000512 | bytes 10000000 | tf_op jit(solution)/shard_map/forward_backward/pallas_call | solution.py:972
  155.3 0.0 copy-done
  155.3 0.0 copy-done.1
  155.3 0.0 copy-done.2
  155.3 0.0 copy-done.3
  155.3 0.0 copy-done.4
  155.3 3.9 %update.1 = (f32[6,128,128]{2,1,0:T(8,128)}, f32[6,128,128]{2,1,0:T(8,128)}, f32[6,128,128]{2,1,0:T(8,128)}, f32[6,128,128]{2,1,0:T(8,128)}, bf16[6,128,128]{2,1...) custom-call(f32[6,128,128]{2,1,0:T(8,128)} %get-tuple-element.27.raw, ...), custom_call_target="tpu_custom_call" | custom-call | tf_op jit(solution)/shard_map/update/pallas_call | solution.py:1078
Async XLA Ops:
  0.7 154.6 %copy-start = (f32[6,128,128]{2,1,0:T(8,128)S(1)}, f32[6,128,128]{2,1,0:T(8,128)}, u32[]{:S(2)}) copy-start(f32[6,128,128]{2,1,0:T(8,128)} %master.1) | copy-start | bytes 1179652
  0.7 154.6 %copy-start.1 = (f32[6,128,128]{2,1,0:T(8,128)S(1)}, f32[6,128,128]{2,1,0:T(8,128)}, u32[]{:S(2)}) copy-start(f32[6,128,128]{2,1,0:T(8,128)} %left_stats.1) | copy-start | bytes 1179652
  0.7 154.6 %copy-start.2 = (f32[6,128,128]{2,1,0:T(8,128)S(1)}, f32[6,128,128]{2,1,0:T(8,128)}, u32[]{:S(2)}) copy-start(f32[6,128,128]{2,1,0:T(8,128)} %right_stats.1) | copy-start | bytes 1179652
  0.7 154.6 %copy-start.3 = (f32[6,128,128]{2,1,0:T(8,128)S(1)}, f32[6,128,128]{2,1,0:T(8,128)}, u32[]{:S(2)}) copy-start(f32[6,128,128]{2,1,0:T(8,128)} %left_root.1) | copy-start | bytes 1179652
  0.7 154.6 %copy-start.4 = (f32[6,128,128]{2,1,0:T(8,128)S(1)}, f32[6,128,128]{2,1,0:T(8,128)}, u32[]{:S(2)}) copy-start(f32[6,128,128]{2,1,0:T(8,128)} %right_root.1) | copy-start | bytes 1179652

commit v5 on v4

--- a/solution.py
+++ b/solution.py
@@ -89,13 +89,25 @@
     return [device(pos, 1 - core)] + [device(moved(pos, a, s), core) for a in range(3) for s in (1, -1)]
 
 
-def announce(semaphore, others):
-    for other in others:
-        pl.semaphore_signal(semaphore, inc=1, device_id=other, device_id_type=MESH)
-
-
-def all_announced(semaphore, others):
-    pl.semaphore_wait(semaphore, len(others))
+def others():
+    pos, core = place()
+    plane = [(i, j, 0, 0) for i in range(4) for j in range(4) if i or j]
+    column = [(0, 0, i, j) for j in range(2) for i in range(4) if i or j]
+    near = [(1, 0, 0, 0), (3, 0, 0, 0), (0, 1, 0, 0), (0, 3, 0, 0), (0, 0, 1, 0), (0, 0, 3, 0), (0, 0, 0, 1)]
+    return [
+        device(tuple((c + by) % 4 for c, by in zip(pos, steps)), core if turn == 0 else 1 - core)
+        for *steps, turn in plane + column
+        if (*steps, turn) not in near
+    ]
+
+
+def announce(semaphore, partners):
+    for partner in partners:
+        pl.semaphore_signal(semaphore, inc=1, device_id=partner, device_id_type=MESH)
+
+
+def all_announced(semaphore, partners):
+    pl.semaphore_wait(semaphore, len(partners))
 
 
 def loop(count, body, together=1):
@@ -281,7 +293,7 @@
 def pass_kernel(
     owner_in, places_in, master_in, vectors_in, patches, keep_in, cotangent, output, input_grad, master, vec_out,
     g, left, right, flats, q, k, v, att, a_low, probs, w_qkv, w_out, wall, sums, vec,
-    vectors, keep, owner, places, made, tables, send_sem, recv_sem, held_sem, ready,
+    vectors, keep, owner, places, made, tables, send_sem, recv_sem, held_sem, ready, ready_too,
 ):
     tokens, d_mid, d_a, mid = (flats.at[i] for i in range(4))
     loads = [
@@ -529,7 +541,7 @@
 
     for copy in sends:
         copy.wait_send()
-    announce(ready, sum(partners(), []))
+    announce(ready, neighbours())
 
     def first_back(j):
         at = lanes(j, 256)
@@ -563,7 +575,10 @@
         if stage == 3:
             output[...] = (mid[...] + vec[7:8, :])[:TOKENS].astype(BF16)
 
-    return heads_back, input_side, output_side
+    def further():
+        announce(ready_too, others())
+
+    return heads_back, input_side, output_side, further
 
 
 ROUNDS = (
@@ -605,7 +620,7 @@
     g, kept, a_out, a_in,
     vec_y, vec_y_in, vec_x, vec_x_in, vec_z, vec_z_in, vec_t, tiles,
     tw_send, tw_recv, c_send, c_recv, b_send, b_recv, a_send, a_recv, v_send, v_recv, n_send, n_recv,
-    heads_back, between,
+    heads_back, between, total_copy,
 ):
     pos, core = place()
     twin = device(pos, 1 - core)
@@ -868,6 +883,7 @@
         total[2 * p] = value[:128]
         total[2 * p + 1] = value[128:]
         squares = squares + by_eights(value * value)
+    total_copy.start()
 
     def norm_copy(stage, i):
         n = 15 * stage + i
@@ -911,34 +927,47 @@
 
 def whole_kernel(
     owner, places, master_in, vectors_in, patches, keep_in, cotangent,
-    output, input_grad, total, window, norm_tile, *scratch,
+    output_out, input_grad_out, total_out, window, norm_tile, *scratch,
 ):
     gathered, scattered = scratch[:PASS_SCRATCH], scratch[PASS_SCRATCH:]
     g, left, right, flats = gathered[:4]
-    vec_in, *scattered = scattered
-    ready = gathered[-1]
-    heads_back, input_side, output_side = pass_kernel(
+    vec_in, output, input_grad, total, out_sem, *scattered = scattered
+    ready, ready_too = gathered[-2:]
+    results = [
+        pltpu.make_async_copy(src, dst, out_sem.at[i])
+        for i, (src, dst) in enumerate(((output, output_out), (input_grad, input_grad_out), (total, total_out)))
+    ]
+    heads_back, input_side, output_side, further = pass_kernel(
         owner, places, master_in, vectors_in, patches, keep_in, cotangent, output, input_grad, total, vec_in, *gathered
     )
 
     def between(k, vec_stage):
         if k < 0:
-            all_announced(ready, sum(partners(), []))
+            all_announced(ready, neighbours())
         elif 1 <= k <= 3:
             input_side(k - 1)
+            if k == 1:
+                further()
             if k == 3:
+                results[1].start()
                 vec_stage(-1)
         elif 4 <= k <= 7:
             output_side(k - 4)
+            if k == 5:
+                all_announced(ready_too, others())
+            if k == 7:
+                results[0].start()
         if k in (5, 7, 9, 11):
             vec_stage((k - 5) // 2)
 
     scatter_kernel(
-        gathered[TABLES], left, right, vec_in, total, window, norm_tile, g, flats, *scattered, heads_back, between
+        gathered[TABLES], left, right, vec_in, total, window, norm_tile, g, flats, *scattered, heads_back, between, results[2]
     )
-
-
-PASS_SCRATCH, TABLES = 25, 20
+    for result in results:
+        result.wait()
+
+
+PASS_SCRATCH, TABLES = 26, 20
 
 
 def forward_backward(*operands):
@@ -967,6 +996,7 @@
         dma((3, 40)),
         dma((8,)),
         pltpu.SemaphoreType.REGULAR,
+        pltpu.SemaphoreType.REGULAR,
     ]
     assert len(pass_scratch) == PASS_SCRATCH
     return pl.pallas_call(
@@ -979,10 +1009,14 @@
             jax.ShapeDtypeStruct((8, 128), F32),
         ],
         in_specs=[pl.BlockSpec(memory_space=pltpu.HBM)] * 7,
-        out_specs=[vmem] * 5,
+        out_specs=[pl.BlockSpec(memory_space=pltpu.HBM)] * 3 + [vmem] * 2,
         scratch_shapes=pass_scratch
         + [
             pltpu.VMEM((2, 8, D), F32),
+            pltpu.VMEM((TOKENS, D), BF16),
+            pltpu.VMEM((TOKENS, D), BF16),
+            pltpu.VMEM((6, SIDE, SIDE), F32),
+            dma((3,)),
             pltpu.VMEM((9, 256, 128), BF16),
             pltpu.VMEM((9, 256, 128), BF16),
             pltpu.VMEM((4, 8, 256), F32),

time: 160 us -> 158 us (0.988)
  no operation moved by 1% of the time
where the time goes in v5:
time: 158 us
  Pallas kernels  157 us (99%)
    pallas_call x1, Pallas kernels, forward_backward(): pl.pallas_call(whole_kernel, out_shape=[jax.ShapeDtypeStruct((TOKENS, D),...  153 us
    pallas_call x1, Pallas kernels, update(): pl.pallas_call(step_kernel, grid=(6 // per,), out_shape=[f32_blocks] * 4...  3.94 us

profile of v5, /device:TPU:1, one launch (start us, length us, event | category | flops | bytes accessed | tf_op | source)
XLA Modules:
  0.0 157.9 jit_solution(14746269927570498919)
XLA Ops:
  0.7 0.0 copy-start
  0.7 0.0 copy-start.1
  0.7 0.0 copy-start.2
  0.7 0.0 copy-start.3
  0.7 0.0 copy-start.4
  0.7 153.0 %forward_backward.1 = (bf16[245,1024]{1,0:T(8,128)(2,1)}, bf16[245,1024]{1,0:T(8,128)(2,1)}, f32[6,128,128]{2,1,0:T(8,128)}, f32[2,8,128]{2,1,0:T(8,128)}, f32[8,128]{1,0:T(8,128)}) custom-call(s32[6,128]{1,0:T(8,128)} %bitcast.11, s32[6,128]{1,0:T(8,128)} %constant.36.clone.places, f32[6,128,128]{2,1,0:T(8,128)} %master.1, f32[8,12]{1,0:T(8,128)} %bitcast.8, ...), custom_call_target="tpu_custom_call" | custom-call | flops 19000000512 | bytes 10000000 | tf_op jit(solution)/shard_map/forward_backward/pallas_call | solution.py:1002
  153.8 0.0 copy-done
  153.8 0.0 copy-done.1
  153.8 0.0 copy-done.2
  153.8 0.0 copy-done.3
  153.8 0.0 copy-done.4
  153.8 3.9 %update.1 = (f32[6,128,128]{2,1,0:T(8,128)}, f32[6,128,128]{2,1,0:T(8,128)}, f32[6,128,128]{2,1,0:T(8,128)}, f32[6,128,128]{2,1,0:T(8,128)}, bf16[6,128,128]{2,1...) custom-call(f32[6,128,128]{2,1,0:T(8,128)} %get-tuple-element.27.raw, ...), custom_call_target="tpu_custom_call" | custom-call | tf_op jit(solution)/shard_map/update/pallas_call | solution.py:1112
Async XLA Ops:
  0.7 153.1 %copy-start = (f32[6,128,128]{2,1,0:T(8,128)S(1)}, f32[6,128,128]{2,1,0:T(8,128)}, u32[]{:S(2)}) copy-start(f32[6,128,128]{2,1,0:T(8,128)} %master.1) | copy-start | bytes 1179652
  0.7 153.1 %copy-start.1 = (f32[6,128,128]{2,1,0:T(8,128)S(1)}, f32[6,128,128]{2,1,0:T(8,128)}, u32[]{:S(2)}) copy-start(f32[6,128,128]{2,1,0:T(8,128)} %left_stats.1) | copy-start | bytes 1179652
  0.7 153.1 %copy-start.2 = (f32[6,128,128]{2,1,0:T(8,128)S(1)}, f32[6,128,128]{2,1,0:T(8,128)}, u32[]{:S(2)}) copy-start(f32[6,128,128]{2,1,0:T(8,128)} %right_stats.1) | copy-start | bytes 1179652
  0.7 153.1 %copy-start.3 = (f32[6,128,128]{2,1,0:T(8,128)S(1)}, f32[6,128,128]{2,1,0:T(8,128)}, u32[]{:S(2)}) copy-start(f32[6,128,128]{2,1,0:T(8,128)} %left_root.1) | copy-start | bytes 1179652
  0.7 153.1 %copy-start.4 = (f32[6,128,128]{2,1,0:T(8,128)S(1)}, f32[6,128,128]{2,1,0:T(8,128)}, u32[]{:S(2)}) copy-start(f32[6,128,128]{2,1,0:T(8,128)} %right_root.1) | copy-start | bytes 1179652

commit v6 on v5

--- a/solution.py
+++ b/solution.py
@@ -945,14 +945,17 @@
         if k < 0:
             all_announced(ready, neighbours())
         elif 1 <= k <= 3:
-            input_side(k - 1)
+            for n in ((), (0,), (1, 2), ())[k]:
+                input_side(n)
             if k == 1:
                 further()
+            if k == 2:
+                results[1].start()
             if k == 3:
-                results[1].start()
                 vec_stage(-1)
         elif 4 <= k <= 7:
-            output_side(k - 4)
+            for n in ((0, 1), (2,), (3,), ())[k - 4]:
+                output_side(n)
             if k == 5:
                 all_announced(ready_too, others())
             if k == 7:

time: 158 us -> 157 us (level)
  no operation moved by 1% of the time
where the time goes in v6:
time: 157 us
  Pallas kernels  156 us (99%)
    pallas_call x1, Pallas kernels, forward_backward(): pl.pallas_call(whole_kernel, out_shape=[jax.ShapeDtypeStruct((TOKENS, D),...  152 us
    pallas_call x1, Pallas kernels, update(): pl.pallas_call(step_kernel, grid=(6 // per,), out_shape=[f32_blocks] * 4...  3.94 us

profile of v6, /device:TPU:1, one launch (start us, length us, event | category | flops | bytes accessed | tf_op | source)
XLA Modules:
  0.0 157.4 jit_solution(15478099589488424793)
XLA Ops:
  0.7 0.0 copy-start
  0.7 0.0 copy-start.1
  0.7 0.0 copy-start.2
  0.7 0.0 copy-start.3
  0.7 0.0 copy-start.4
  0.7 152.5 %forward_backward.1 = (bf16[245,1024]{1,0:T(8,128)(2,1)}, bf16[245,1024]{1,0:T(8,128)(2,1)}, f32[6,128,128]{2,1,0:T(8,128)}, f32[2,8,128]{2,1,0:T(8,128)}, f32[8,128]{1,0:T(8,128)}) custom-call(s32[6,128]{1,0:T(8,128)} %bitcast.11, s32[6,128]{1,0:T(8,128)} %constant.36.clone.places, f32[6,128,128]{2,1,0:T(8,128)} %master.1, f32[8,12]{1,0:T(8,128)} %bitcast.8, ...), custom_call_target="tpu_custom_call" | custom-call | flops 19000000512 | bytes 10000000 | tf_op jit(solution)/shard_map/forward_backward/pallas_call | solution.py:1005
  153.2 0.0 copy-done
  153.2 0.0 copy-done.1
  153.2 0.0 copy-done.2
  153.2 0.0 copy-done.3
  153.2 0.0 copy-done.4
  153.2 3.9 %update.1 = (f32[6,128,128]{2,1,0:T(8,128)}, f32[6,128,128]{2,1,0:T(8,128)}, f32[6,128,128]{2,1,0:T(8,128)}, f32[6,128,128]{2,1,0:T(8,128)}, bf16[6,128,128]{2,1...) custom-call(f32[6,128,128]{2,1,0:T(8,128)} %get-tuple-element.27.raw, ...), custom_call_target="tpu_custom_call" | custom-call | tf_op jit(solution)/shard_map/update/pallas_call | solution.py:1115
Async XLA Ops:
  0.7 152.5 %copy-start = (f32[6,128,128]{2,1,0:T(8,128)S(1)}, f32[6,128,128]{2,1,0:T(8,128)}, u32[]{:S(2)}) copy-start(f32[6,128,128]{2,1,0:T(8,128)} %master.1) | copy-start | bytes 1179652
  0.7 152.5 %copy-start.1 = (f32[6,128,128]{2,1,0:T(8,128)S(1)}, f32[6,128,128]{2,1,0:T(8,128)}, u32[]{:S(2)}) copy-start(f32[6,128,128]{2,1,0:T(8,128)} %left_stats.1) | copy-start | bytes 1179652
  0.7 152.5 %copy-start.2 = (f32[6,128,128]{2,1,0:T(8,128)S(1)}, f32[6,128,128]{2,1,0:T(8,128)}, u32[]{:S(2)}) copy-start(f32[6,128,128]{2,1,0:T(8,128)} %right_stats.1) | copy-start | bytes 1179652
  0.7 152.5 %copy-start.3 = (f32[6,128,128]{2,1,0:T(8,128)S(1)}, f32[6,128,128]{2,1,0:T(8,128)}, u32[]{:S(2)}) copy-start(f32[6,128,128]{2,1,0:T(8,128)} %left_root.1) | copy-start | bytes 1179652
  0.7 152.5 %copy-start.4 = (f32[6,128,128]{2,1,0:T(8,128)S(1)}, f32[6,128,128]{2,1,0:T(8,128)}, u32[]{:S(2)}) copy-start(f32[6,128,128]{2,1,0:T(8,128)} %right_root.1) | copy-start | bytes 1179652
